TPU v7x, 32 devices: a whole 2x2x4 slice. The times are simulated.
32 devices in a mesh: gx: 4 (over z), gy: 4 (over y, x), gz: 2 (over core).
Axes of the slice: x: 2, y: 2, z: 4, core: 2. Of those that a mesh axis runs over, the one named last changes fastest.
Arguments:
- rhs_boxes: float32 [2, 64, 32768], P('gz', ('gx', 'gy')), may hold values from -18 to 18
- a_boxes: float32 [2, 64, 32768], P('gz', ('gx', 'gy')), may hold values from 0.05 to 0.5
- b_boxes: float32 [2, 64, 32768], P('gz', ('gx', 'gy')), may hold values from 0.2 to 2
- new_place: int32 [2, 64], P('gz', ('gx', 'gy')), may hold values from 0 to 63, as said below
Outputs:
- solution: float32 [256, 128, 128], P('gx', 'gy', 'gz')
- residual: float32 [256, 128, 128], P('gx', 'gy', 'gz')
Inputs may be any that keep to these rules, and one draw needn't show every extreme that they name: `new_place`: each entry is p = t * 4 + q: the box goes to device t of its layer (counted in the order of the gx+gy axes) at box position q. The entries of one layer are a permutation of its positions. The boxes of one device go to 4 different devices.
All inputs are finite; a program needn't handle non-finite values.
Results may differ from a plain program's by a relative error of at most 0.000079.
Values sent between devices are 32-bit elements; how exact they have to be, the bound alone decides.
A program may use at most 192 MiB of HBM per device.

v0:
```python
import jax
import jax.numpy as jnp
from jax import lax
from jax.sharding import PartitionSpec as P

BOX_EDGE = 32
BOXES_Z = 2
SWEEPS = 1
COARSE_SWEEPS = 4


def with_halo(cells, sides, width):
    for axis, dim in sides:
        count = lax.axis_size(axis)
        ends = count - 1
        head = lax.slice_in_dim(cells, 0, width, axis=dim)
        tail = lax.slice_in_dim(cells, cells.shape[dim] - width, cells.shape[dim], axis=dim)
        cells = jnp.concatenate(
            [
                lax.ppermute(tail, axis, [(i, (i + 1) % count) for i in range(ends)]),
                cells,
                lax.ppermute(head, axis, [((i + 1) % count, i) for i in range(ends)]),
            ],
            axis=dim,
        )
    return cells


def stencil_sum(padded, across_x, across_y, across_z):
    summed = across_x[:-1] * padded[:-2, 1:-1, 1:-1] + across_x[1:] * padded[2:, 1:-1, 1:-1]
    summed = (
        summed
        + across_y[:, :-1] * padded[1:-1, :-2, 1:-1]
        + across_y[:, 1:] * padded[1:-1, 2:, 1:-1]
    )
    summed = (
        summed
        + across_z[:, :, :-1] * padded[1:-1, 1:-1, :-2]
        + across_z[:, :, 1:] * padded[1:-1, 1:-1, 2:]
    )
    return summed


def face_total(across_x, across_y, across_z):
    return (
        across_x[:-1]
        + across_x[1:]
        + across_y[:, :-1]
        + across_y[:, 1:]
        + across_z[:, :, :-1]
        + across_z[:, :, 1:]
    )


def checker(extent):
    return (
        lax.broadcasted_iota(jnp.int32, extent, 0)
        + lax.broadcasted_iota(jnp.int32, extent, 1)
        + lax.broadcasted_iota(jnp.int32, extent, 2)
    ) % 2


def fine_pad(values):
    return with_halo(values, (("gx", 0), ("gy", 1), ("gz", 2)), 1)


def coarse_pad(values):
    return with_halo(values, (("gx", 0), ("gy", 1), ("gz", 2)), 1)


def colour_sweeps(solution, source, coeffs, sweeps, padder):
    diagonal, across_x, across_y, across_z, weight = coeffs
    colour = checker(solution.shape)
    for repeat in range(sweeps):
        for current in (0, 1):
            padded = padder(solution)
            updated = (
                source + weight * stencil_sum(padded, across_x, across_y, across_z)
            ) / diagonal
            solution = jnp.where(colour == current, updated, solution)
    return solution


def misfit(solution, source, coeffs):
    diagonal, across_x, across_y, across_z, weight = coeffs
    padded = fine_pad(solution)
    return source - (
        diagonal * solution - weight * stencil_sum(padded, across_x, across_y, across_z)
    )


def restrict(values):
    size_x, size_y, size_z = values.shape
    return values.reshape(size_x // 2, 2, size_y // 2, 2, size_z // 2, 2).mean(axis=(1, 3, 5))


def coarse_faces(across_x, across_y, across_z):
    size_x, size_y, size_z = (across_x.shape[0] - 1, across_x.shape[1], across_x.shape[2])
    coarse_x = (
        across_x[0::2].reshape(size_x // 2 + 1, size_y // 2, 2, size_z // 2, 2).mean(axis=(2, 4))
    )
    coarse_y = (
        across_y[:, 0::2].reshape(size_x // 2, 2, size_y // 2 + 1, size_z // 2, 2).mean(axis=(1, 4))
    )
    coarse_z = (
        across_z[:, :, 0::2]
        .reshape(size_x // 2, 2, size_y // 2, 2, size_z // 2 + 1)
        .mean(axis=(1, 3))
    )
    return (coarse_x, coarse_y, coarse_z)


def prolong(values):
    size_x, size_y, size_z = values.shape
    spread = jnp.broadcast_to(values[:, None, :, None, :, None], (size_x, 2, size_y, 2, size_z, 2))
    return spread.reshape(2 * size_x, 2 * size_y, 2 * size_z)


def to_brick(boxes):
    shaped = boxes.reshape(2, BOXES_Z, BOX_EDGE, BOX_EDGE, BOX_EDGE)
    return shaped.transpose(0, 2, 3, 1, 4).reshape(2 * BOX_EDGE, BOX_EDGE, BOXES_Z * BOX_EDGE)


def body(rhs_boxes, a_boxes, b_boxes, new_place):
    members = lax.axis_size(("gx", "gy"))
    box_count = new_place.shape[1]
    capacity = 1
    slot_count = members * capacity
    target = new_place[0] // box_count
    position = new_place[0] % box_count
    send_slot = target * capacity
    chosen = (
        lax.broadcasted_iota(jnp.int32, (slot_count, box_count), 0) == send_slot[None, :]
    ).astype(jnp.int32)
    source = jnp.sum(chosen * lax.broadcasted_iota(jnp.int32, (slot_count, box_count), 1), axis=1)
    filled = jnp.sum(chosen, axis=1) > 0
    send_rhs = jnp.where(filled[:, None], rhs_boxes[0][source], 0.0)
    send_a = jnp.where(filled[:, None], a_boxes[0][source], 0.0)
    send_b = jnp.where(filled[:, None], b_boxes[0][source], 0.0)
    send_position = jnp.where(filled, position[source], -1)
    got_rhs, got_a, got_b, got_position = (
        lax.all_to_all(send_rhs, ("gx", "gy"), split_axis=0, concat_axis=0, tiled=True),
        lax.all_to_all(send_a, ("gx", "gy"), split_axis=0, concat_axis=0, tiled=True),
        lax.all_to_all(send_b, ("gx", "gy"), split_axis=0, concat_axis=0, tiled=True),
        lax.all_to_all(send_position, ("gx", "gy"), split_axis=0, concat_axis=0, tiled=True),
    )
    wanted = (
        lax.broadcasted_iota(jnp.int32, (box_count, slot_count), 0) == got_position[None, :]
    ).astype(jnp.int32)
    picked = jnp.sum(wanted * lax.broadcasted_iota(jnp.int32, (box_count, slot_count), 1), axis=1)
    rhs = to_brick(got_rhs[picked])
    acoef = to_brick(got_a[picked])
    bcoef = to_brick(got_b[picked])
    padded_b = with_halo(bcoef, (("gx", 0), ("gy", 1), ("gz", 2)), 1)
    across_x = 0.5 * (padded_b[1:, 1:-1, 1:-1] + padded_b[:-1, 1:-1, 1:-1])
    across_y = 0.5 * (padded_b[1:-1, 1:, 1:-1] + padded_b[1:-1, :-1, 1:-1])
    across_z = 0.5 * (padded_b[1:-1, 1:-1, 1:] + padded_b[1:-1, 1:-1, :-1])
    diagonal = acoef + 1.0 * face_total(across_x, across_y, across_z)

    def smooth(solution):
        return colour_sweeps(
            solution, rhs, (diagonal, across_x, across_y, across_z, 1.0), SWEEPS, fine_pad
        )

    fine_level = (diagonal, across_x, across_y, across_z, 1.0)
    smoothed = smooth(jnp.zeros_like(rhs))
    coarse_rhs = restrict(misfit(smoothed, rhs, fine_level))
    coarse_x, coarse_y, coarse_z = coarse_faces(across_x, across_y, across_z)
    coarse = (
        restrict(acoef) + 0.25 * face_total(coarse_x, coarse_y, coarse_z),
        coarse_x,
        coarse_y,
        coarse_z,
        0.25,
    )
    correction = colour_sweeps(
        jnp.zeros_like(coarse_rhs), coarse_rhs, coarse, COARSE_SWEEPS, coarse_pad
    )
    solution = smooth(smoothed + prolong(correction))
    return (solution, misfit(solution, rhs, fine_level))


def solution(mesh):
    return jax.shard_map(
        body,
        mesh=mesh,
        in_specs=(
            P("gz", ("gx", "gy"), None),
            P("gz", ("gx", "gy"), None),
            P("gz", ("gx", "gy"), None),
            P("gz", ("gx", "gy")),
        ),
        out_specs=(P("gx", "gy", "gz"), P("gx", "gy", "gz")),
        check_vma=False,
    )
```

profile of v0, /device:TPU:0, one launch (start us, length us, event | category | flops | bytes accessed | tf_op | source)
XLA Modules:
  0.0 827.9 jit_solution(16613199069990204298)
XLA Ops:
  3.5 8.3 %all-to-all-start.1 = ((s32[16,1,1]{2,1,0:T(1,128)}), s32[16,1,1]{2,1,0:T(1,128)S(1)}, u32[]{:S(2)}, u32[]{:S(2)}) async-start(s32[16,1,1]{2,1,0:T(1,128)} %copy.200), calls=%async_computation.1 | async-start | bytes 16384 | tf_op jit(solution)/shard_map/all_to_all | solution.py:145
  19.3 4.7 bitcast_select_fusion.1
  27.6 7.0 all-to-all-start.2
  34.5 5.1 copy.214
  39.6 37.7 %all-to-all-done.2 = f32[16,1,32768]{2,1,0:T(1,128)} async-done(((f32[16,1,32768]{2,1,0:T(1,128)}), f32[16,1,32768]{2,1,0:T(1,128)}, u32[]{:S(2)}, u32[]{:S(2)}) %all-to-all-start.2) | async-done | bytes 2097184 | tf_op jit(solution)/shard_map/all_to_all | solution.py:144
  77.4 9.8 %all-to-all-start.3 = ((f32[16,1,32768]{2,1,0:T(1,128)}), f32[16,1,32768]{2,1,0:T(1,128)}, u32[]{:S(2)}, u32[]{:S(2)}) async-start(f32[16,1,32768]{2,1,0:T(1,128)} %copy.214), calls=%async_computation.3 | async-start | bytes 4194304 | tf_op jit(solution)/shard_map/all_to_all | solution.py:143
  90.7 39.1 %all-to-all-done.3 = f32[16,1,32768]{2,1,0:T(1,128)} async-done(((f32[16,1,32768]{2,1,0:T(1,128)}), f32[16,1,32768]{2,1,0:T(1,128)}, u32[]{:S(2)}, u32[]{:S(2)}) %all-to-all-start.3) | async-done | bytes 2097184 | tf_op jit(solution)/shard_map/all_to_all | solution.py:143
  129.8 9.6 %all-to-all-start = ((f32[16,1,32768]{2,1,0:T(1,128)}), f32[16,1,32768]{2,1,0:T(1,128)}, u32[]{:S(2)}, u32[]{:S(2)}) async-start(f32[16,1,32768]{2,1,0:T(1,128)} %copy.199), calls=%async_computation | async-start | bytes 4194304 | tf_op jit(solution)/shard_map/all_to_all | solution.py:142
  144.6 4.5 collective-permute-start.24
  150.9 22.0 %collective-permute-done.2 = f32[1,32,64]{2,1,0:T(8,128)S(1)} collective-permute-done((f32[1,32,64]{2,1,0:T(8,128)S(1)}, f32[1,32,64]{2,1,0:T(8,128)S(1)}, u32[]{:S(2)}, u32[]{:S(2)}) %collective-permute-start.2) | collective-permute-done | bytes 8224 | tf_op jit(solution)/shard_map/ppermute | solution.py:20
  196.0 16.7 %collective-permute-start.1 = (f32[1,32,64]{2,1,0:T(8,128)S(1)}, f32[1,32,64]{2,1,0:T(8,128)S(1)}, u32[]{:S(2)}, u32[]{:S(2)}) collective-permute-start(f32[1,32,64]{2,1,0:T(8,128)S(1)} %copy.206), channel_id=1, source_target_pairs={{0,8},{8,16},{16,24},{1,9},{9,17},{17,25},{2,10},{10,18},{18,26},{... | collective-permute-start | bytes 24584 | tf_op jit(solution)/shard_map/ppermute | solution.py:20
  252.3 5.7 collective-permute-start.5
  267.5 13.9 %collective-permute-start.11 = (f32[66,34,1]{0,2,1:T(1,128)S(1)}, f32[66,34,1]{0,2,1:T(1,128)S(1)}, u32[]{:S(2)}, u32[]{:S(2)}) collective-permute-start(f32[66,34,1]{0,2,1:T(1,128)S(1)} %get-tuple-element.29), channel_id=1, source_target_pairs={{1,0},{3,2},{5,4},{7,6},{9,8},{11,10},{13,12},{15,14},{17,16},{19,... | collective-permute-start | bytes 26936 | tf_op jit(solution)/shard_map/ppermute | solution.py:22
  282.8 5.3 fusion.77
  298.3 4.8 collective-permute-start.26
  308.3 5.4 collective-permute-start.14
  315.4 5.1 collective-permute-done.15
  332.4 21.8 %reshape_reshape.3 = f32[32,2,16,2,32,2]{3,2,5,4,1,0:T(8,128)} reshape(f32[2,32,32,2,32]{2,4,3,1,0:T(8,128)} %bitcast.58) | data formatting | bytes 1048576 | tf_op jit(solution)/shard_map/reshape;reshape | solution.py:94
  354.2 12.2 %reduce_sum.85 = f32[32,16,32]{1,2,0:T(8,128)S(1)} reduce(f32[32,2,16,2,32,2]{3,2,5,4,1,0:T(8,128)} %reshape_reshape.3, f32[]{:T(128)} %constant.81.clone.1), dimensions={1,3,5}, to_apply=%region_7.8 | reduce | flops 114688 | bytes 589828 | tf_op jit(solution)/shard_map/reduce_sum | solution.py:94
  367.3 10.0 %slice.793 = f32[33,32,64]{0,2,1:T(8,128)} slice(f32[65,32,64]{0,2,1:T(8,128)S(1)} %fusion.84), slice={[0:65:2], [0:32:1], [0:64:1]} | slice | bytes 540672 | tf_op jit(solution)/shard_map/slice | solution.py:100
  379.6 14.0 %fusion.63 = f32[64,32,64]{0,2,1:T(8,128)S(1)} fusion(f32[64,32,64]{0,2,1:T(8,128)} %copy-done.26, f32[64,32,64]{0,2,1:T(8,128)} %reshape.171, f32[66,34,1]{0,2,1:T(1,128)S(1)} %collective-permute-done.17, f32[66,1,64]{0,2,1:T(8,128)S(1)} %collective-permute-done.15, f32[66,1,64]{0,2,1:T(8,128)S(1)} %collective-permute-done.14, f32[1,32,64]{0,2,1:T(8,128)} %copy.220, ...), kind=kLoop, calls=%fused_computation.168 | loop fusion | flops 6815744 | bytes 5311008 | tf_op jit(solution)/shard_map/jit(_where)/select_n | solution.py:80
  396.9 5.2 collective-permute-start.18
  418.0 4.8 collective-permute-start.20
  441.7 10.7 %fusion.49 = f32[64,32,64]{0,2,1:T(8,128)} fusion(f32[64,32,64]{0,2,1:T(8,128)} %reshape.171, f32[66,34,1]{0,2,1:T(1,128)S(1)} %collective-permute-done.23, f32[66,1,64]{0,2,1:T(8,128)S(1)} %collective-permute-done.21, f32[66,1,64]{0,2,1:T(8,128)S(1)} %collective-permute-done.20, f32[1,32,64]{0,2,1:T(8,128)} %copy.226, f32[64,32,64]{0,2,1:T(8,128)S(1)} %copy-done.11, ...), kind=kLoop, calls=%fused_computation.136 | loop fusion | flops 4980736 | bytes 5311008 | tf_op jit(solution)/shard_map/sub | solution.py:87
  455.4 36.8 %reshape.176 = f32[32,2,16,2,32,2]{5,4,3,2,1,0:T(8,128)} reshape(f32[64,32,64]{2,1,0:T(8,128)} %copy.229) | data formatting | bytes 1048576 | tf_op jit(solution)/shard_map/reshape | solution.py:94
  492.2 12.2 %reduce_sum.81 = f32[32,16,32]{2,1,0:T(8,128)S(1)} reduce(f32[32,2,16,2,32,2]{5,4,3,2,1,0:T(8,128)} %reshape.176, f32[]{:T(128)} %constant.81.clone.1), dimensions={1,3,5}, to_apply=%region_3.4 | reduce | flops 114688 | bytes 589828 | tf_op jit(solution)/shard_map/reduce_sum | solution.py:94
  666.6 11.4 %broadcast_in_dim.53 = f32[32,2,16,2,32,2]{5,4,3,2,1,0:T(8,128)} broadcast(f32[32,16,32]{2,1,0:T(8,128)S(1)} %fusion.103), dimensions={0,2,4} | broadcast | bytes 589824 | tf_op jit(solution)/shard_map/broadcast_in_dim | solution.py:115
  678.0 28.6 %reshape.180 = f32[64,32,64]{2,1,0:T(8,128)} reshape(f32[32,2,16,2,32,2]{5,4,3,2,1,0:T(8,128)} %broadcast_in_dim.53) | data formatting | bytes 1048576 | tf_op jit(solution)/shard_map/reshape | solution.py:116
  730.4 4.4 collective-permute-done.75
  740.4 5.7 fusion.36
  775.6 5.7 fusion.22
  811.0 13.7 %fusion.8 = f32[64,32,64]{0,2,1:T(8,128)} fusion(f32[64,32,64]{0,2,1:T(8,128)} %reshape.171, f32[66,34,1]{0,2,1:T(1,128)S(1)} %collective-permute-done.89, f32[66,1,64]{0,2,1:T(8,128)S(1)} %collective-permute-done.87, f32[66,1,64]{0,2,1:T(8,128)S(1)} %collective-permute-done.86, f32[1,32,64]{0,2,1:T(8,128)} %copy.251, f32[64,32,64]{0,2,1:T(8,128)} %copy-done.12, ...), kind=kLoop, calls=%fused_computation.41 | loop fusion | flops 4980736 | bytes 5311008 | tf_op jit(solution)/shard_map/sub | solution.py:87
  (411 shorter events, 423.0 us)
Async XLA Ops:
  3.5 24.1 %all-to-all-start.1 = ((s32[16,1,1]{2,1,0:T(1,128)}), s32[16,1,1]{2,1,0:T(1,128)S(1)}, u32[]{:S(2)}, u32[]{:S(2)}) async-start(s32[16,1,1]{2,1,0:T(1,128)} %copy.200), calls=%async_computation.1 | async-start | bytes 16384 | tf_op jit(solution)/shard_map/all_to_all | solution.py:145
  27.6 49.8 %all-to-all-start.2 = ((f32[16,1,32768]{2,1,0:T(1,128)}), f32[16,1,32768]{2,1,0:T(1,128)}, u32[]{:S(2)}, u32[]{:S(2)}) async-start(f32[16,1,32768]{2,1,0:T(1,128)} %copy.202), calls=%async_computation.2 | async-start | bytes 4194304 | tf_op jit(solution)/shard_map/all_to_all | solution.py:144
  77.4 52.5 %all-to-all-start.3 = ((f32[16,1,32768]{2,1,0:T(1,128)}), f32[16,1,32768]{2,1,0:T(1,128)}, u32[]{:S(2)}, u32[]{:S(2)}) async-start(f32[16,1,32768]{2,1,0:T(1,128)} %copy.214), calls=%async_computation.3 | async-start | bytes 4194304 | tf_op jit(solution)/shard_map/all_to_all | solution.py:143
  129.8 102.0 %all-to-all-start = ((f32[16,1,32768]{2,1,0:T(1,128)}), f32[16,1,32768]{2,1,0:T(1,128)}, u32[]{:S(2)}, u32[]{:S(2)}) async-start(f32[16,1,32768]{2,1,0:T(1,128)} %copy.199), calls=%async_computation | async-start | bytes 4194304 | tf_op jit(solution)/shard_map/all_to_all | solution.py:142
  139.5 33.4 %collective-permute-start.2 = (f32[1,32,64]{2,1,0:T(8,128)S(1)}, f32[1,32,64]{2,1,0:T(8,128)S(1)}, u32[]{:S(2)}, u32[]{:S(2)}) collective-permute-start(f32[1,32,64]{2,1,0:T(8,128)S(1)} %broadcast.216), channel_id=1, source_target_pairs={{0,8},{8,16},{16,24},{1,9},{9,17},{17,25},{2,10},{10,18},{18,26},{... | collective-permute-start | bytes 24584 | tf_op jit(solution)/shard_map/ppermute | solution.py:20
  143.2 30.1 %collective-permute-start.3 = (f32[1,32,64]{2,1,0:T(8,128)S(1)}, f32[1,32,64]{2,1,0:T(8,128)S(1)}, u32[]{:S(2)}, u32[]{:S(2)}) collective-permute-start(f32[1,32,64]{2,1,0:T(8,128)S(1)} %broadcast.216), channel_id=1, source_target_pairs={{8,0},{16,8},{24,16},{9,1},{17,9},{25,17},{10,2},{18,10},{26,18},{... | collective-permute-start | bytes 24584 | tf_op jit(solution)/shard_map/ppermute | solution.py:22
  144.6 153.6 %collective-permute-start.24 = (f32[1,16,32]{2,1,0:T(8,128)S(1)}, f32[1,16,32]{2,1,0:T(8,128)S(1)}, u32[]{:S(2)}, u32[]{:S(2)}) collective-permute-start(f32[1,16,32]{2,1,0:T(8,128)S(1)} %broadcast.219), channel_id=1, source_target_pairs={{0,8},{8,16},{16,24},{1,9},{9,17},{17,25},{2,10},{10,18},{18,26},{... | collective-permute-start | bytes 6152 | tf_op jit(solution)/shard_map/ppermute | solution.py:20
  149.1 149.1 %collective-permute-start.25 = (f32[1,16,32]{2,1,0:T(8,128)S(1)}, f32[1,16,32]{2,1,0:T(8,128)S(1)}, u32[]{:S(2)}, u32[]{:S(2)}) collective-permute-start(f32[1,16,32]{2,1,0:T(8,128)S(1)} %broadcast.219), channel_id=1, source_target_pairs={{8,0},{16,8},{24,16},{9,1},{17,9},{25,17},{10,2},{18,10},{26,18},{... | collective-permute-start | bytes 6152 | tf_op jit(solution)/shard_map/ppermute | solution.py:22
  175.1 21.0 %collective-permute-start.6 = (f32[66,1,64]{0,2,1:T(8,128)S(1)}, f32[66,1,64]{0,2,1:T(8,128)S(1)}, u32[]{:S(2)}, u32[]{:S(2)}) collective-permute-start(f32[66,1,64]{0,2,1:T(8,128)S(1)} %get-tuple-element.42), channel_id=1, source_target_pairs={{0,2},{2,4},{4,6},{1,3},{3,5},{5,7},{8,10},{10,12},{12,14},{9,11},... | collective-permute-start | bytes 50696 | tf_op jit(solution)/shard_map/ppermute | solution.py:20
  178.7 34.1 %collective-permute-start.7 = (f32[66,1,64]{0,2,1:T(8,128)S(1)}, f32[66,1,64]{0,2,1:T(8,128)S(1)}, u32[]{:S(2)}, u32[]{:S(2)}) collective-permute-start(f32[66,1,64]{0,2,1:T(8,128)S(1)} %get-tuple-element.43), channel_id=1, source_target_pairs={{2,0},{4,2},{6,4},{3,1},{5,3},{7,5},{10,8},{12,10},{14,12},{11,9},... | collective-permute-start | bytes 50696 | tf_op jit(solution)/shard_map/ppermute | solution.py:22
  193.1 55.1 %collective-permute-start = (f32[1,32,64]{2,1,0:T(8,128)S(1)}, f32[1,32,64]{2,1,0:T(8,128)S(1)}, u32[]{:S(2)}, u32[]{:S(2)}) collective-permute-start(f32[1,32,64]{2,1,0:T(8,128)S(1)} %copy.204), channel_id=1, source_target_pairs={{8,0},{16,8},{24,16},{9,1},{17,9},{25,17},{10,2},{18,10},{26,18},{... | collective-permute-start | bytes 24584 | tf_op jit(solution)/shard_map/ppermute | solution.py:22
  196.0 52.6 %collective-permute-start.1 = (f32[1,32,64]{2,1,0:T(8,128)S(1)}, f32[1,32,64]{2,1,0:T(8,128)S(1)}, u32[]{:S(2)}, u32[]{:S(2)}) collective-permute-start(f32[1,32,64]{2,1,0:T(8,128)S(1)} %copy.206), channel_id=1, source_target_pairs={{0,8},{8,16},{16,24},{1,9},{9,17},{17,25},{2,10},{10,18},{18,26},{... | collective-permute-start | bytes 24584 | tf_op jit(solution)/shard_map/ppermute | solution.py:20
  214.1 68.6 %collective-permute-start.10 = (f32[66,34,1]{0,2,1:T(1,128)S(1)}, f32[66,34,1]{0,2,1:T(1,128)S(1)}, u32[]{:S(2)}, u32[]{:S(2)}) collective-permute-start(f32[66,34,1]{0,2,1:T(1,128)S(1)} %get-tuple-element.28), channel_id=1, source_target_pairs={{0,1},{2,3},{4,5},{6,7},{8,9},{10,11},{12,13},{14,15},{16,17},{18,... | collective-permute-start | bytes 26936 | tf_op jit(solution)/shard_map/ppermute | solution.py:20
  251.0 8.9 %collective-permute-start.4 = (f32[66,1,64]{0,2,1:T(8,128)S(1)}, f32[66,1,64]{0,2,1:T(8,128)S(1)}, u32[]{:S(2)}, u32[]{:S(2)}) collective-permute-start(f32[66,1,64]{0,2,1:T(8,128)S(1)} %get-tuple-element.41), channel_id=1, source_target_pairs={{2,0},{4,2},{6,4},{3,1},{5,3},{7,5},{10,8},{12,10},{14,12},{11,9},... | collective-permute-start | bytes 50696 | tf_op jit(solution)/shard_map/ppermute | solution.py:22
  252.3 7.6 collective-permute-start.5
  260.1 7.3 collective-permute-start.8
  261.5 20.0 %collective-permute-start.9 = (f32[66,34,1]{0,2,1:T(1,128)S(1)}, f32[66,34,1]{0,2,1:T(1,128)S(1)}, u32[]{:S(2)}, u32[]{:S(2)}) collective-permute-start(f32[66,34,1]{0,2,1:T(1,128)S(1)} %get-tuple-element.27), channel_id=1, source_target_pairs={{0,1},{2,3},{4,5},{6,7},{8,9},{10,11},{12,13},{14,15},{16,17},{18,... | collective-permute-start | bytes 26936 | tf_op jit(solution)/shard_map/ppermute | solution.py:20
  267.5 15.3 %collective-permute-start.11 = (f32[66,34,1]{0,2,1:T(1,128)S(1)}, f32[66,34,1]{0,2,1:T(1,128)S(1)}, u32[]{:S(2)}, u32[]{:S(2)}) collective-permute-start(f32[66,34,1]{0,2,1:T(1,128)S(1)} %get-tuple-element.29), channel_id=1, source_target_pairs={{1,0},{3,2},{5,4},{7,6},{9,8},{11,10},{13,12},{15,14},{17,16},{19,... | collective-permute-start | bytes 26936 | tf_op jit(solution)/shard_map/ppermute | solution.py:22
  291.4 13.1 %collective-permute-start.12 = (f32[1,32,64]{2,1,0:T(8,128)S(1)}, f32[1,32,64]{2,1,0:T(8,128)S(1)}, u32[]{:S(2)}, u32[]{:S(2)}) collective-permute-start(f32[1,32,64]{2,1,0:T(8,128)S(1)} %copy.217), channel_id=1, source_target_pairs={{0,8},{8,16},{16,24},{1,9},{9,17},{17,25},{2,10},{10,18},{18,26},{... | collective-permute-start | bytes 24584 | tf_op jit(solution)/shard_map/ppermute | solution.py:20
  296.9 9.0 %collective-permute-start.13 = (f32[1,32,64]{2,1,0:T(8,128)S(1)}, f32[1,32,64]{2,1,0:T(8,128)S(1)}, u32[]{:S(2)}, u32[]{:S(2)}) collective-permute-start(f32[1,32,64]{2,1,0:T(8,128)S(1)} %copy.219), channel_id=1, source_target_pairs={{8,0},{16,8},{24,16},{9,1},{17,9},{25,17},{10,2},{18,10},{26,18},{... | collective-permute-start | bytes 24584 | tf_op jit(solution)/shard_map/ppermute | solution.py:22
  298.3 16.8 %collective-permute-start.26 = (f32[34,1,32]{2,1,0:T(1,128)S(1)}, f32[34,1,32]{2,1,0:T(1,128)S(1)}, u32[]{:S(2)}, u32[]{:S(2)}) collective-permute-start(f32[34,1,32]{2,1,0:T(1,128)S(1)} %get-tuple-element.86), channel_id=1, source_target_pairs={{0,2},{2,4},{4,6},{1,3},{3,5},{5,7},{8,10},{10,12},{12,14},{9,11},... | collective-permute-start | bytes 13064 | tf_op jit(solution)/shard_map/ppermute | solution.py:20
  303.1 12.0 %collective-permute-start.27 = (f32[34,1,32]{2,1,0:T(1,128)S(1)}, f32[34,1,32]{2,1,0:T(1,128)S(1)}, u32[]{:S(2)}, u32[]{:S(2)}) collective-permute-start(f32[34,1,32]{2,1,0:T(1,128)S(1)} %get-tuple-element.87), channel_id=1, source_target_pairs={{2,0},{4,2},{6,4},{3,1},{5,3},{7,5},{10,8},{12,10},{14,12},{11,9},... | collective-permute-start | bytes 13064 | tf_op jit(solution)/shard_map/ppermute | solution.py:22
  308.3 7.0 collective-permute-start.14
  313.8 6.7 collective-permute-start.15
  320.7 58.8 %collective-permute-start.16 = (f32[66,34,1]{0,2,1:T(1,128)S(1)}, f32[66,34,1]{0,2,1:T(1,128)S(1)}, u32[]{:S(2)}, u32[]{:S(2)}) collective-permute-start(f32[66,34,1]{0,2,1:T(1,128)S(1)} %get-tuple-element.24), channel_id=1, source_target_pairs={{0,1},{2,3},{4,5},{6,7},{8,9},{10,11},{12,13},{14,15},{16,17},{18,... | collective-permute-start | bytes 26936 | tf_op jit(solution)/shard_map/ppermute | solution.py:20
  322.0 57.6 %collective-permute-start.17 = (f32[66,34,1]{0,2,1:T(1,128)S(1)}, f32[66,34,1]{0,2,1:T(1,128)S(1)}, u32[]{:S(2)}, u32[]{:S(2)}) collective-permute-start(f32[66,34,1]{0,2,1:T(1,128)S(1)} %get-tuple-element.25), channel_id=1, source_target_pairs={{1,0},{3,2},{5,4},{7,6},{9,8},{11,10},{13,12},{15,14},{17,16},{19,... | collective-permute-start | bytes 26936 | tf_op jit(solution)/shard_map/ppermute | solution.py:22
  324.4 180.0 %collective-permute-start.28 = (f32[34,18,1]{2,1,0:T(8,128)}, f32[34,18,1]{2,1,0:T(8,128)}, u32[]{:S(2)}, u32[]{:S(2)}) collective-permute-start(f32[34,18,1]{2,1,0:T(8,128)} %get-tuple-element.70), channel_id=1, source_target_pairs={{0,1},{2,3},{4,5},{6,7},{8,9},{10,11},{12,13},{14,15},{16,17},{18,... | collective-permute-start | bytes 7352 | tf_op jit(solution)/shard_map/ppermute | solution.py:20
  328.2 176.2 %collective-permute-start.29 = (f32[34,18,1]{2,1,0:T(8,128)}, f32[34,18,1]{2,1,0:T(8,128)}, u32[]{:S(2)}, u32[]{:S(2)}) collective-permute-start(f32[34,18,1]{2,1,0:T(8,128)} %get-tuple-element.71), channel_id=1, source_target_pairs={{1,0},{3,2},{5,4},{7,6},{9,8},{11,10},{13,12},{15,14},{17,16},{19,... | collective-permute-start | bytes 7352 | tf_op jit(solution)/shard_map/ppermute | solution.py:22
  396.9 16.0 %collective-permute-start.18 = (f32[1,32,64]{2,1,0:T(8,128)S(1)}, f32[1,32,64]{2,1,0:T(8,128)}, u32[]{:S(2)}, u32[]{:S(2)}) collective-permute-start(f32[1,32,64]{2,1,0:T(8,128)S(1)} %copy.223), channel_id=1, source_target_pairs={{0,8},{8,16},{16,24},{1,9},{9,17},{17,25},{2,10},{10,18},{18,26},{... | collective-permute-start | bytes 24584 | tf_op jit(solution)/shard_map/ppermute | solution.py:20
  404.2 10.7 %collective-permute-start.19 = (f32[1,32,64]{2,1,0:T(8,128)}, f32[1,32,64]{2,1,0:T(8,128)}, u32[]{:S(2)}, u32[]{:S(2)}) collective-permute-start(f32[1,32,64]{2,1,0:T(8,128)} %copy.225), channel_id=1, source_target_pairs={{8,0},{16,8},{24,16},{9,1},{17,9},{25,17},{10,2},{18,10},{26,18},{... | collective-permute-start | bytes 24584 | tf_op jit(solution)/shard_map/ppermute | solution.py:22
  418.0 15.8 %collective-permute-start.20 = (f32[66,1,64]{0,2,1:T(8,128)S(1)}, f32[66,1,64]{0,2,1:T(8,128)S(1)}, u32[]{:S(2)}, u32[]{:S(2)}) collective-permute-start(f32[66,1,64]{0,2,1:T(8,128)S(1)} %get-tuple-element.36), channel_id=1, source_target_pairs={{0,2},{2,4},{4,6},{1,3},{3,5},{5,7},{8,10},{10,12},{12,14},{9,11},... | collective-permute-start | bytes 50696 | tf_op jit(solution)/shard_map/ppermute | solution.py:20
  422.9 11.0 %collective-permute-start.21 = (f32[66,1,64]{0,2,1:T(8,128)S(1)}, f32[66,1,64]{0,2,1:T(8,128)S(1)}, u32[]{:S(2)}, u32[]{:S(2)}) collective-permute-start(f32[66,1,64]{0,2,1:T(8,128)S(1)} %get-tuple-element.37), channel_id=1, source_target_pairs={{2,0},{4,2},{6,4},{3,1},{5,3},{7,5},{10,8},{12,10},{14,12},{11,9},... | collective-permute-start | bytes 50696 | tf_op jit(solution)/shard_map/ppermute | solution.py:22
  (110 other events, 809.9 us)
where the time goes:
time: 835 us; the launch traced here: 828 us
  local copies, waits for them, and re-layouts  250 us (30%)
  starting transfers between devices  246 us (29%)
  waiting for transfers between devices  208 us (25%)
  other arithmetic  121 us (14%)
    ppermute x45, starting transfers between devices, with_halo(): lax.ppermute(tail, axis, [(i, (i + 1) % count) for i in range(ends)])  138 us
    ppermute x45, waiting for transfers between devices, with_halo(): lax.ppermute(head, axis, [((i + 1) % count, i) for i in range(ends)])  107 us
    ppermute x45, starting transfers between devices, with_halo(): lax.ppermute(head, axis, [((i + 1) % count, i) for i in range(ends)])  72.5 us
    all_to_all x1, waiting for transfers between devices, body(): lax.all_to_all(send_a, ('gx', 'gy'), split_axis=0, concat_axis=0, tiled=T...  39.1 us
    all_to_all x1, waiting for transfers between devices, body(): lax.all_to_all(send_b, ('gx', 'gy'), split_axis=0, concat_axis=0, tiled=T...  37.7 us
    select_n x12, other arithmetic, colour_sweeps(): solution = jnp.where(colour == current, updated, solution)  37.5 us
    reshape x1, local copies, waits for them, and re-layouts, restrict(): values.reshape(size_x // 2, 2, size_y // 2, 2, size_z // 2, 2)  36.8 us
    reshape x2, local copies, waits for them, and re-layouts, prolong(): return spread.reshape(2 * size_x, 2 * size_y, 2 * size_z)  31.3 us
  transfers between devices with their start and end apart: 94, of which 43 were waited for; matrix products, arithmetic and copies ran while one was open for 32% of the time, Pallas kernels for 0%

commit v1 on v0

v1 whole, which is shorter than its diff:
```python
import functools

import jax
import jax.numpy as jnp
from jax import lax
from jax.experimental import pallas as pl
from jax.experimental.pallas import tpu as pltpu
from jax.sharding import PartitionSpec as P

MESH = pl.DeviceIdType.MESH
NX, NY, NZ = 64, 32, 64
LANES = 128
COARSE_HALVES = 8
EXCHANGES = 13
F32 = jnp.float32


def lane_ids():
    return lax.broadcasted_iota(jnp.int32, (NY, LANES), 1)


def row_ids():
    return lax.broadcasted_iota(jnp.int32, (NY, LANES), 0)


def pair_z(v):
    return v + jnp.where(lane_ids() % 2 == 0, pltpu.roll(v, LANES - 1, 1), pltpu.roll(v, 1, 1))


def pair_y(v):
    return v + jnp.where(row_ids() % 2 == 0, pltpu.roll(v, NY - 1, 0), pltpu.roll(v, 1, 0))


def even_y(v):
    return jnp.where(row_ids() % 2 == 0, v, pltpu.roll(v, 1, 0))


def odd_y(v):
    return jnp.where(row_ids() % 2 == 1, v, pltpu.roll(v, NY - 1, 0))


def even_z(v):
    return jnp.where(lane_ids() % 2 == 0, v, pltpu.roll(v, 1, 1))


def odd_z(v):
    return jnp.where(lane_ids() % 2 == 1, v, pltpu.roll(v, LANES - 1, 1))


def kernel(
    sizes,
    place_ref, rhs_in, a_in, b_in,
    sol_out, res_out,
    got_place, inv_vmem, inv_smem, got_b, got_a, got_rhs, sorted_, final,
    bv, rh, ac, dg, rd, fx, fyl, fyh, fzl, fzh, v,
    cc, cf, crd, cfx, cfyl, cfyh, cfzl, cfzh,
    hx, hy, hz, ys, zs,
    place_send, place_recv, send1, recv1, send2, recv2, inv_sem, halo_send, halo_recv,
):
    n_gx, n_gy, n_gz = sizes
    members = n_gx * n_gy
    rows = 256 // members
    slabs = rows // 8
    gx, gy, gz = lax.axis_index("gx"), lax.axis_index("gy"), lax.axis_index("gz")
    me = gx * n_gy + gy
    got = (got_b, got_a, got_rhs)

    def member(t):
        return (t // n_gy, t % n_gy, gz)

    @pl.loop(0, EXCHANGES)
    def _(e):
        for side in range(2):
            hx[e, side] = jnp.zeros((NY, LANES), F32)
            hy[e, side] = jnp.zeros((NX, LANES), F32)
            hz[e, side] = jnp.zeros((NY, LANES), F32)

    barrier = pltpu.get_barrier_semaphore()

    @pl.loop(1, members)
    def _(k):
        pl.semaphore_signal(barrier, inc=1, device_id=member((me + k) % members), device_id_type=MESH)

    @pl.when(gz > 0)
    def _():
        pl.semaphore_signal(barrier, inc=1, device_id=(gx, gy, gz - 1), device_id_type=MESH)

    @pl.when(gz < n_gz - 1)
    def _():
        pl.semaphore_signal(barrier, inc=1, device_id=(gx, gy, gz + 1), device_id_type=MESH)

    pl.semaphore_wait(
        barrier, members - 1 + (gz > 0).astype(jnp.int32) + (gz < n_gz - 1).astype(jnp.int32)
    )

    def place_copy(peer, k, slot):
        return pltpu.make_async_remote_copy(
            src_ref=place_ref, dst_ref=got_place.at[slot],
            send_sem=place_send.at[k], recv_sem=place_recv.at[slot],
            device_id=member(peer), device_id_type=MESH,
        )

    def copy1(f, peer, k, slot):
        return pltpu.make_async_remote_copy(
            src_ref=(b_in, a_in, rhs_in)[f].at[pl.ds(pl.multiple_of(peer * 4 * rows, 8), 4 * rows)],
            dst_ref=got[f].at[slot],
            send_sem=send1.at[f, k], recv_sem=recv1.at[f, slot],
            device_id=member(peer), device_id_type=MESH,
        )

    def copy2(f, peer, k, slot):
        return pltpu.make_async_remote_copy(
            src_ref=sorted_.at[f, peer], dst_ref=final.at[f, slot],
            send_sem=send2.at[f, k], recv_sem=recv2.at[f, slot],
            device_id=member(peer), device_id_type=MESH,
        )

    @pl.loop(1, members)
    def _(k):
        place_copy((me + k) % members, k, me).start()

    for f in range(3):
        @pl.loop(1, members)
        def _(k):
            copy1(f, (me + k) % members, k, me).start()

    got_place[me] = place_ref[...]
    for f in range(3):
        got[f][me] = (b_in, a_in, rhs_in)[f][pl.ds(pl.multiple_of(me * 4 * rows, 8), 4 * rows), :]

    @pl.loop(1, members)
    def _(k):
        place_copy((me + k) % members, k, (me + k) % members).wait_recv()

    lane8 = lax.broadcasted_iota(jnp.int32, (8, LANES), 1)
    row8 = lax.broadcasted_iota(jnp.int32, (8, LANES), 0)

    def find(src, total):
        here = (got_place[src] == lane8) & (row8 < 4)
        return jnp.maximum(total, jnp.where(here, src * 4 + row8, 0))

    owner = lax.fori_loop(0, members, find, jnp.zeros((8, LANES), jnp.int32))
    for shift in (4, 2, 1):
        owner = jnp.maximum(owner, pltpu.roll(owner, shift, 0))
    inv_vmem[...] = owner
    inv_copy = pltpu.make_async_copy(inv_vmem, inv_smem, inv_sem)
    inv_copy.start()
    inv_copy.wait()

    def forward(f):
        @pl.loop(1, members)
        def _(k):
            copy1(f, (me + k) % members, k, (me + k) % members).wait_recv()

        def pick(t, q):
            index = inv_smem[0, t * 4 + q]
            return got[f][index >> 2, pl.ds(index & 3, rows, stride=4), :]

        @pl.loop(1, members)
        def _(k):
            t = (me + k) % members
            for q in range(4):
                sorted_[f, t, q * rows:(q + 1) * rows, :] = pick(t, q)
            copy2(f, t, k, me).start()

        for q in range(4):
            final[f, me, q * rows:(q + 1) * rows, :] = pick(me, q)

    def unpack(f, out, first):
        @pl.loop(1, members)
        def _(k):
            copy2(f, (me + k) % members, k, (me + k) % members).wait_recv()

        @pl.loop(0, members)
        def _(j):
            for qx in range(2):
                for slab in range(slabs):
                    low = qx * 2 * rows + slab * 8
                    t0 = final[f, j, low:low + 8, :]
                    t1 = final[f, j, low + rows:low + rows + 8, :]
                    x = qx * 32 + j * slabs + slab
                    for yr in range(4):
                        r0 = pltpu.roll(t0, (LANES - 32 * yr) % LANES, 1)
                        r1 = pltpu.roll(t1, (LANES + 32 - 32 * yr) % LANES, 1)
                        out[x + first, pl.ds(yr, 8, stride=4), :] = jnp.where(lane8 < 32, r0, r1)

    def exchange(e, field, planes):
        for act in ("start", "wait"):
            for axis in range(3):
                for side in range(2):
                    d = axis * 2 + side
                    place, count = ((gx, n_gx), (gy, n_gy), (gz, n_gz))[axis]
                    there = place > 0 if side == 0 else place < count - 1
                    other = [gx, gy, gz]
                    other[axis] = place + (2 * side - 1)
                    if axis == 0:
                        src, dst = field.at[1 if side == 0 else planes], hx
                        to, mine = dst.at[e, 1 - side], dst.at[e, side]
                    elif axis == 1:
                        src = ys.at[side, pl.ds(0, planes)]
                        to, mine = hy.at[e, 1 - side, pl.ds(0, planes)], hy.at[e, side, pl.ds(0, planes)]
                    else:
                        src, to, mine = zs, hz.at[e, 1 - side], hz.at[e, side]

                    @pl.when(there)
                    def _():
                        out = pltpu.make_async_remote_copy(
                            src_ref=src, dst_ref=to, send_sem=halo_send.at[d],
                            recv_sem=halo_recv.at[e, axis * 2 + 1 - side],
                            device_id=tuple(other), device_id_type=MESH,
                        )
                        if act == "start":
                            out.start()
                        else:
                            out.wait_send()
                            pltpu.make_async_remote_copy(
                                src_ref=src, dst_ref=mine, send_sem=halo_send.at[d],
                                recv_sem=halo_recv.at[e, d],
                                device_id=tuple(other), device_id_type=MESH,
                            ).wait_recv()
        field[0] = hx[e, 0]
        field[planes + 1] = hx[e, 1]

    def stage(n, x, st, packed):
        ys[0, pl.ds(x, 1), :] = n[0:1, :]
        ys[1, pl.ds(x, 1), :] = n[NY - 1:NY, :]
        group = lane_ids() // st
        top = pltpu.roll(n, (x * st + LANES - (NZ - st)) % LANES, 1)
        bottom = pltpu.roll(n, (x * st + 64) % LANES, 1)
        return jnp.where(group == x, top, jnp.where(group == x + 64 // st, bottom, packed))

    def beside(field, e, x, st):
        c = field[x + 1]
        lane, row = lane_ids(), row_ids()
        yl = jnp.where(row < st, hy[e, 0, pl.ds(x, 1), :], pltpu.roll(c, st, 0))
        yh = jnp.where(row >= NY - st, hy[e, 1, pl.ds(x, 1), :], pltpu.roll(c, NY - st, 0))
        low = pltpu.roll(hz[e, 0], (2 * LANES - st - x * st) % LANES, 1)
        high = pltpu.roll(hz[e, 1], (LANES - x * st) % LANES, 1)
        w = jnp.where(lane >= LANES - st, low, jnp.where(lane >= NZ, high, c))
        return c, field[x], field[x + 2], yl, yh, pltpu.roll(w, st, 1), pltpu.roll(w, LANES - st, 1)

    def fine_nb(e, x):
        c, xl, xh, yl, yh, zl, zh = beside(v, e, x, 1)
        return c, (
            (fx[x] * xl + fx[x + 1] * xh) + (fyl[x] * yl + fyh[x] * yh) + (fzl[x] * zl + fzh[x] * zh)
        )

    def coarse_nb(e, x):
        c, xl, xh, yl, yh, zl, zh = beside(cc, e, x, 2)
        return c, (
            (cfx[x] * xl + cfx[x + 1] * xh) + (cfyl[x] * yl + cfyh[x] * yh) + (cfzl[x] * zl + cfzh[x] * zh)
        )

    def sweep(planes, body):
        zs[...] = lax.fori_loop(0, planes, body, jnp.zeros((NY, LANES), F32))

    def is_colour(x, st, colour):
        return (row_ids() // st + lane_ids() // st + x + colour) % 2 == 0

    forward(0)
    forward(1)
    unpack(0, bv, 1)
    sweep(NX, lambda x, packed: stage(bv[x + 1], x, 1, packed))
    exchange(0, bv, NX)
    forward(2)

    @pl.loop(0, NX)
    def _(x):
        c, xl, xh, yl, yh, zl, zh = beside(bv, 0, x, 1)
        fx[x] = 0.5 * (c + xl)
        fyl[x] = 0.5 * (c + yl)
        fyh[x] = 0.5 * (c + yh)
        fzl[x] = 0.5 * (c + zl)
        fzh[x] = 0.5 * (c + zh)

    fx[NX] = 0.5 * (bv[NX] + bv[NX + 1])

    unpack(1, ac, 0)

    @pl.loop(0, NX // 2)
    def _(i):
        x = 2 * i
        for o in range(2):
            d = ac[x + o] + (
                (fx[x + o] + fx[x + o + 1]) + (fyl[x + o] + fyh[x + o]) + (fzl[x + o] + fzh[x + o])
            )
            dg[x + o] = d
            rd[x + o] = 1.0 / d
        s = 0.0625
        wxl = s * pair_z(pair_y(fx[x]))
        wxh = s * pair_z(pair_y(fx[x + 2]))
        wyl = s * pair_z(even_y(fyl[x] + fyl[x + 1]))
        wyh = s * pair_z(odd_y(fyh[x] + fyh[x + 1]))
        wzl = s * pair_y(even_z(fzl[x] + fzl[x + 1]))
        wzh = s * pair_y(odd_z(fzh[x] + fzh[x + 1]))
        cfx[i] = wxl
        cfx[i + 1] = wxh
        cfyl[i] = wyl
        cfyh[i] = wyh
        cfzl[i] = wzl
        cfzh[i] = wzh
        ca = 0.125 * pair_z(pair_y(ac[x] + ac[x + 1]))
        crd[i] = 1.0 / (ca + ((wxl + wxh) + (wyl + wyh) + (wzl + wzh)))

    unpack(2, rh, 0)

    def first_red(x, packed):
        n = jnp.where(is_colour(x, 1, 0), rh[x] * rd[x], 0.0)
        v[x + 1] = n
        return stage(n, x, 1, packed)

    def half(e, colour, staged):
        def step(x, packed):
            c, nb = fine_nb(e, x)
            n = jnp.where(is_colour(x, 1, colour), (rh[x] + nb) * rd[x], c)
            v[x + 1] = n
            return stage(n, x, 1, packed)

        sweep(NX, step)

    sweep(NX, first_red)
    exchange(1, v, NX)
    half(1, 1, True)
    exchange(2, v, NX)

    def first_coarse(i, packed):
        total = None
        for o in range(2):
            c, nb = fine_nb(2, 2 * i + o)
            r = rh[2 * i + o] - (dg[2 * i + o] * c - nb)
            total = r if total is None else total + r
        f = 0.125 * pair_z(pair_y(total))
        cf[i] = f
        n = jnp.where(is_colour(i, 2, 0), f * crd[i], 0.0)
        cc[i + 1] = n
        return stage(n, i, 2, packed)

    sweep(NX // 2, first_coarse)

    @pl.loop(1, COARSE_HALVES)
    def _(h):
        e = 2 + h
        exchange(e, cc, NX // 2)

        def step(i, packed):
            c, nb = coarse_nb(e, i)
            n = jnp.where(is_colour(i, 2, h), (cf[i] + nb) * crd[i], c)
            cc[i + 1] = n
            return stage(n, i, 2, packed)

        sweep(NX // 2, step)

    def correct(i, packed):
        c = cc[i + 1]
        for o in range(2):
            n = v[2 * i + o + 1] + c
            v[2 * i + o + 1] = n
            packed = stage(n, 2 * i + o, 1, packed)
        return packed

    sweep(NX // 2, correct)
    exchange(10, v, NX)
    half(10, 0, True)
    exchange(11, v, NX)
    half(11, 1, True)
    exchange(12, v, NX)

    @pl.loop(0, NX)
    def _(x):
        c, nb = fine_nb(12, x)
        sol_out[x] = c[:, :NZ]
        res_out[x] = (rh[x] - (dg[x] * c - nb))[:, :NZ]

    @pl.loop(1, members)
    def _(k):
        peer = (me + k) % members
        place_copy(peer, k, me).wait_send()
        for f in range(3):
            copy1(f, peer, k, me).wait_send()
            copy2(f, peer, k, me).wait_send()


def solution(mesh):
    sizes = (mesh.shape["gx"], mesh.shape["gy"], mesh.shape["gz"])
    members = sizes[0] * sizes[1]
    rows = 256 // members

    def rows128(boxes):
        return boxes[0].reshape(4, 256, LANES).transpose(1, 0, 2).reshape(1024, LANES)

    def body(rhs_boxes, a_boxes, b_boxes, new_place):
        spot = jnp.where(jnp.arange(8)[:, None] < 4, jnp.tile(new_place[0], 2)[:, None], -1)
        spot = jnp.broadcast_to(spot, (8, LANES)).astype(jnp.int32)
        fine = pltpu.VMEM((NX, NY, LANES), F32)
        coarse = pltpu.VMEM((NX // 2, NY, LANES), F32)
        box = pltpu.VMEM((members, 4 * rows, LANES), F32)
        boxes = pltpu.VMEM((3, members, 4 * rows, LANES), F32)
        dma = pltpu.SemaphoreType.DMA
        return pl.pallas_call(
            functools.partial(kernel, sizes),
            out_shape=[jax.ShapeDtypeStruct((NX, NY, NZ), F32)] * 2,
            in_specs=[pl.BlockSpec(memory_space=pltpu.VMEM)] * 4,
            out_specs=[pl.BlockSpec(memory_space=pltpu.VMEM)] * 2,
            scratch_shapes=[
                pltpu.VMEM((members, 8, LANES), jnp.int32),
                pltpu.VMEM((8, LANES), jnp.int32),
                pltpu.SMEM((8, LANES), jnp.int32),
                box, box, box, boxes, boxes,
                pltpu.VMEM((NX + 2, NY, LANES), F32),
                fine, fine, fine, fine,
                pltpu.VMEM((NX + 1, NY, LANES), F32),
                fine, fine, fine, fine,
                pltpu.VMEM((NX + 2, NY, LANES), F32),
                pltpu.VMEM((NX // 2 + 2, NY, LANES), F32),
                coarse, coarse,
                pltpu.VMEM((NX // 2 + 1, NY, LANES), F32),
                coarse, coarse, coarse, coarse,
                pltpu.VMEM((EXCHANGES, 2, NY, LANES), F32),
                pltpu.VMEM((EXCHANGES, 2, NX, LANES), F32),
                pltpu.VMEM((EXCHANGES, 2, NY, LANES), F32),
                pltpu.VMEM((2, NX, LANES), F32),
                pltpu.VMEM((NY, LANES), F32),
                dma((members,)), dma((members,)),
                dma((3, members)), dma((3, members)),
                dma((3, members)), dma((3, members)),
                dma,
                dma((6,)), dma((EXCHANGES, 6)),
            ],
            compiler_params=pltpu.CompilerParams(
                collective_id=0, has_side_effects=True, vmem_limit_bytes=48 * 1024 * 1024
            ),
        )(spot, rows128(rhs_boxes), rows128(a_boxes), rows128(b_boxes))

    return jax.shard_map(
        body,
        mesh=mesh,
        in_specs=(
            P("gz", ("gx", "gy"), None),
            P("gz", ("gx", "gy"), None),
            P("gz", ("gx", "gy"), None),
            P("gz", ("gx", "gy")),
        ),
        out_specs=(P("gx", "gy", "gz"), P("gx", "gy", "gz")),
        check_vma=False,
    )
```

time: 835 us -> 261 us (0.31)
  Pallas kernels: 0 us -> 254 us
  starting transfers between devices: 246 us -> 0 us
  local copies, waits for them, and re-layouts: 250 us -> 5.87 us
  waiting for transfers between devices: 208 us -> 0 us
  other arithmetic: 121 us -> 0.01 us
    pallas_call x0 -> x1, Pallas kernels: none -> 254 us  [body(): pl.pallas_call(functools.partial(kernel, sizes), out_shape=[jax.ShapeDtyp...]
    ppermute x90 -> x0, starting transfers between devices: 211 us -> none  [the longest x45 138 us: with_halo(): lax.ppermute(tail, axis, [(i, (i + 1) % count) for i in range(ends)])]
    ppermute x90 -> x0, waiting for transfers between devices: 131 us -> none  [the longest x45 107 us: with_halo(): lax.ppermute(head, axis, [((i + 1) % count, i) for i in range(ends)])]
    reshape x10 -> x0, local copies, waits for them, and re-layouts: 85.1 us -> none  [the longest x1 36.8 us: restrict(): values.reshape(size_x // 2, 2, size_y // 2, 2, size_z // 2, 2)]
    all_to_all x4 -> x0, waiting for transfers between devices: 76.8 us -> none  [the longest x1 39.1 us: body(): lax.all_to_all(send_a, ('gx', 'gy'), split_axis=0, concat_axis=0, tiled=T...]
    slice x38 -> x0, local copies, waits for them, and re-layouts: 52.3 us -> none  [the longest x27 22 us: with_halo(): lax.slice_in_dim(cells, cells.shape[dim] - width, cells.shape[dim], axis=...]
    select_n x17 -> x1, other arithmetic: 42.9 us -> 0.01 us  [body(): jnp.where(jnp.arange(8)[:, None] < 4, jnp.tile(new_place[0], 2)[:, None],...]
    all_to_all x4 -> x0, starting transfers between devices: 34.7 us -> none  [the longest x1 9.76 us: body(): lax.all_to_all(send_a, ('gx', 'gy'), split_axis=0, concat_axis=0, tiled=T...]
  transfers between devices with their start and end apart: 94 -> 0, of which waited for: 43 -> 0; matrix products, arithmetic and copies ran while one was open for 32% -> 0% of each run, Pallas kernels for 0% -> 0%
where the time goes in v1:
time: 261 us
  Pallas kernels  254 us (97%)
  local copies, waits for them, and re-layouts  5.87 us (2%)
    pallas_call x1, Pallas kernels, body(): pl.pallas_call(functools.partial(kernel, sizes), out_shape=[jax.ShapeDtyp...  254 us
    unnamed x10, local copies, waits for them, and re-layouts  5.71 us

profile of v1, /device:TPU:0, one launch (start us, length us, event | category | flops | bytes accessed | tf_op | source)
XLA Modules:
  0.0 260.6 jit_solution(2720847398792648377)
XLA Ops:
  0.6 0.0 copy-start.3
  0.6 0.6 copy-done.3
  1.3 0.1 broadcast_in_dim_tile.3
  1.4 0.1 broadcast_in_dim.11.place_ref
  1.5 0.0 copy-start
  1.5 1.0 copy-done
  2.5 0.0 copy-start.1
  2.5 1.0 copy-done.1
  3.5 0.0 copy-start.2
  3.5 1.0 copy-done.2
  4.6 254.0 %shard_map.59 = (f32[64,32,64]{2,1,0:T(8,128)S(1)}, f32[64,32,64]{2,1,0:T(8,128)S(1)}) custom-call(s32[8,128]{1,0:T(8,128)S(1)} %broadcast_in_dim.11.place_ref, f32[1024,128]{1,0:T(8,128)S(1)} %bitcast.16, f32[1024,128]{1,0:T(8,128)S(1)} %bitcast.17, f32[1024,128]{1,0:T(8,128)S(1)} %bitcast.18), custom_call_target="tpu_custom_call" | custom-call | tf_op jit(solution)/shard_map/pallas_call | solution.py:399
  258.6 1.0 copy.11
  259.6 1.0 copy.12
  (2 shorter events, 0.0 us)
Async XLA Ops:
  0.6 0.7 copy-start.3
  1.5 1.0 copy-start
  2.5 1.0 copy-start.1
  3.5 1.0 copy-start.2

commit v2 on v1

--- a/solution.py
+++ b/solution.py
@@ -12,6 +12,7 @@
 LANES = 128
 COARSE_HALVES = 8
 EXCHANGES = 13
+GROUP = 4
 F32 = jnp.float32
 
 
@@ -73,7 +74,7 @@
         for side in range(2):
             hx[e, side] = jnp.zeros((NY, LANES), F32)
             hy[e, side] = jnp.zeros((NX, LANES), F32)
-            hz[e, side] = jnp.zeros((NY, LANES), F32)
+            hz[e, side] = jnp.zeros((2, NY, LANES), F32)
 
     barrier = pltpu.get_barrier_semaphore()
 
@@ -221,58 +222,82 @@
         field[0] = hx[e, 0]
         field[planes + 1] = hx[e, 1]
 
-    def stage(n, x, st, packed):
-        ys[0, pl.ds(x, 1), :] = n[0:1, :]
-        ys[1, pl.ds(x, 1), :] = n[NY - 1:NY, :]
-        group = lane_ids() // st
-        top = pltpu.roll(n, (x * st + LANES - (NZ - st)) % LANES, 1)
-        bottom = pltpu.roll(n, (x * st + 64) % LANES, 1)
-        return jnp.where(group == x, top, jnp.where(group == x + 64 // st, bottom, packed))
-
-    def beside(field, e, x, st):
-        c = field[x + 1]
+    def level_pass(planes, st, body, staged=True, field=None, e=None):
+        half_planes = planes // 2
+        spot = ((lane_ids() + st) % LANES) // st
         lane, row = lane_ids(), row_ids()
-        yl = jnp.where(row < st, hy[e, 0, pl.ds(x, 1), :], pltpu.roll(c, st, 0))
-        yh = jnp.where(row >= NY - st, hy[e, 1, pl.ds(x, 1), :], pltpu.roll(c, NY - st, 0))
-        low = pltpu.roll(hz[e, 0], (2 * LANES - st - x * st) % LANES, 1)
-        high = pltpu.roll(hz[e, 1], (LANES - x * st) % LANES, 1)
-        w = jnp.where(lane >= LANES - st, low, jnp.where(lane >= NZ, high, c))
-        return c, field[x], field[x + 2], yl, yh, pltpu.roll(w, st, 1), pltpu.roll(w, LANES - st, 1)
-
-    def fine_nb(e, x):
-        c, xl, xh, yl, yh, zl, zh = beside(v, e, x, 1)
+        for h in range(2):
+            if e is not None:
+                beyond = jnp.where(spot < 48 // st, hz[e, 0, h], hz[e, 1, h])
+
+            def step(g, packed):
+                near = [g * GROUP + i for i in range(GROUP)]
+                xs = [h * half_planes + n for n in near]
+                hoods = [None] * GROUP
+                if e is not None:
+                    loaded = [field[xs[0] + i] for i in range(GROUP + 2)]
+                    hoods = []
+                    for i in range(GROUP):
+                        c = loaded[i + 1]
+                        yl = jnp.where(row < st, hy[e, 0, pl.ds(xs[i], 1), :], pltpu.roll(c, st, 0))
+                        yh = jnp.where(
+                            row >= NY - st, hy[e, 1, pl.ds(xs[i], 1), :], pltpu.roll(c, NY - st, 0)
+                        )
+                        w = jnp.where(
+                            lane >= NZ, pltpu.roll(beyond, (LANES - near[i] * st) % LANES, 1), c
+                        )
+                        zl, zh = pltpu.roll(w, st, 1), pltpu.roll(w, LANES - st, 1)
+                        hoods.append((c, loaded[i], loaded[i + 2], yl, yh, zl, zh))
+                results = body(xs, hoods)
+                if staged:
+                    for i in range(GROUP):
+                        n = results[i]
+                        turned = pltpu.roll(n, (near[i] * st + 64) % LANES, 1)
+                        mine = (spot == near[i]) | (spot == near[i] + 64 // st + 1)
+                        packed = jnp.where(mine, turned, packed)
+                    for i in range(GROUP):
+                        ys[0, pl.ds(xs[i], 1), :] = results[i][0:1, :]
+                        ys[1, pl.ds(xs[i], 1), :] = results[i][NY - 1:NY, :]
+                    return packed
+                return packed
+
+            steps = half_planes // GROUP
+            if staged:
+                zs[h] = lax.fori_loop(0, steps, step, jnp.zeros((NY, LANES), F32))
+            else:
+                lax.fori_loop(0, steps, step, 0)
+
+    def fine_nb(x, hood):
+        c, xl, xh, yl, yh, zl, zh = hood
         return c, (
             (fx[x] * xl + fx[x + 1] * xh) + (fyl[x] * yl + fyh[x] * yh) + (fzl[x] * zl + fzh[x] * zh)
         )
 
-    def coarse_nb(e, x):
-        c, xl, xh, yl, yh, zl, zh = beside(cc, e, x, 2)
+    def coarse_nb(x, hood):
+        c, xl, xh, yl, yh, zl, zh = hood
         return c, (
             (cfx[x] * xl + cfx[x + 1] * xh) + (cfyl[x] * yl + cfyh[x] * yh) + (cfzl[x] * zl + cfzh[x] * zh)
         )
 
-    def sweep(planes, body):
-        zs[...] = lax.fori_loop(0, planes, body, jnp.zeros((NY, LANES), F32))
-
     def is_colour(x, st, colour):
         return (row_ids() // st + lane_ids() // st + x + colour) % 2 == 0
 
     forward(0)
     forward(1)
     unpack(0, bv, 1)
-    sweep(NX, lambda x, packed: stage(bv[x + 1], x, 1, packed))
+    level_pass(NX, 1, lambda xs, hoods: [bv[x + 1] for x in xs])
     exchange(0, bv, NX)
     forward(2)
 
-    @pl.loop(0, NX)
-    def _(x):
-        c, xl, xh, yl, yh, zl, zh = beside(bv, 0, x, 1)
-        fx[x] = 0.5 * (c + xl)
-        fyl[x] = 0.5 * (c + yl)
-        fyh[x] = 0.5 * (c + yh)
-        fzl[x] = 0.5 * (c + zl)
-        fzh[x] = 0.5 * (c + zh)
-
+    def faces(xs, hoods):
+        for x, (c, xl, xh, yl, yh, zl, zh) in zip(xs, hoods):
+            fx[x] = 0.5 * (c + xl)
+            fyl[x] = 0.5 * (c + yl)
+            fyh[x] = 0.5 * (c + yh)
+            fzl[x] = 0.5 * (c + zl)
+            fzh[x] = 0.5 * (c + zh)
+
+    level_pass(NX, 1, faces, staged=False, field=bv, e=0)
     fx[NX] = 0.5 * (bv[NX] + bv[NX + 1])
 
     unpack(1, ac, 0)
@@ -304,72 +329,77 @@
 
     unpack(2, rh, 0)
 
-    def first_red(x, packed):
-        n = jnp.where(is_colour(x, 1, 0), rh[x] * rd[x], 0.0)
-        v[x + 1] = n
-        return stage(n, x, 1, packed)
-
-    def half(e, colour, staged):
-        def step(x, packed):
-            c, nb = fine_nb(e, x)
-            n = jnp.where(is_colour(x, 1, colour), (rh[x] + nb) * rd[x], c)
-            v[x + 1] = n
-            return stage(n, x, 1, packed)
-
-        sweep(NX, step)
-
-    sweep(NX, first_red)
+    def store(field, xs, values):
+        for x, n in zip(xs, values):
+            field[x + 1] = n
+        return values
+
+    def first_red(xs, hoods):
+        return store(v, xs, [jnp.where(is_colour(x, 1, 0), rh[x] * rd[x], 0.0) for x in xs])
+
+    def half(e, colour):
+        def update(xs, hoods):
+            values = []
+            for x, hood in zip(xs, hoods):
+                c, nb = fine_nb(x, hood)
+                values.append(jnp.where(is_colour(x, 1, colour), (rh[x] + nb) * rd[x], c))
+            return store(v, xs, values)
+
+        level_pass(NX, 1, update, field=v, e=e)
+
+    level_pass(NX, 1, first_red)
     exchange(1, v, NX)
-    half(1, 1, True)
+    half(1, 1)
     exchange(2, v, NX)
 
-    def first_coarse(i, packed):
-        total = None
-        for o in range(2):
-            c, nb = fine_nb(2, 2 * i + o)
-            r = rh[2 * i + o] - (dg[2 * i + o] * c - nb)
-            total = r if total is None else total + r
-        f = 0.125 * pair_z(pair_y(total))
-        cf[i] = f
-        n = jnp.where(is_colour(i, 2, 0), f * crd[i], 0.0)
-        cc[i + 1] = n
-        return stage(n, i, 2, packed)
-
-    sweep(NX // 2, first_coarse)
+    def restrict(xs, hoods):
+        for p in range(0, GROUP, 2):
+            total = None
+            for x, hood in zip(xs[p:p + 2], hoods[p:p + 2]):
+                c, nb = fine_nb(x, hood)
+                r = rh[x] - (dg[x] * c - nb)
+                total = r if total is None else total + r
+            cf[xs[p] // 2] = 0.125 * pair_z(pair_y(total))
+
+    level_pass(NX, 1, restrict, staged=False, field=v, e=2)
+
+    def first_coarse(xs, hoods):
+        return store(cc, xs, [jnp.where(is_colour(x, 2, 0), cf[x] * crd[x], 0.0) for x in xs])
+
+    level_pass(NX // 2, 2, first_coarse)
 
     @pl.loop(1, COARSE_HALVES)
     def _(h):
         e = 2 + h
         exchange(e, cc, NX // 2)
 
-        def step(i, packed):
-            c, nb = coarse_nb(e, i)
-            n = jnp.where(is_colour(i, 2, h), (cf[i] + nb) * crd[i], c)
-            cc[i + 1] = n
-            return stage(n, i, 2, packed)
-
-        sweep(NX // 2, step)
-
-    def correct(i, packed):
-        c = cc[i + 1]
-        for o in range(2):
-            n = v[2 * i + o + 1] + c
-            v[2 * i + o + 1] = n
-            packed = stage(n, 2 * i + o, 1, packed)
-        return packed
-
-    sweep(NX // 2, correct)
+        def update(xs, hoods):
+            values = []
+            for x, hood in zip(xs, hoods):
+                c, nb = coarse_nb(x, hood)
+                values.append(jnp.where(is_colour(x, 2, h), (cf[x] + nb) * crd[x], c))
+            return store(cc, xs, values)
+
+        level_pass(NX // 2, 2, update, field=cc, e=e)
+
+    def correct(xs, hoods):
+        coarse = [cc[xs[p] // 2 + 1] for p in range(0, GROUP, 2)]
+        return store(v, xs, [v[x + 1] + coarse[i // 2] for i, x in enumerate(xs)])
+
+    level_pass(NX, 1, correct)
     exchange(10, v, NX)
-    half(10, 0, True)
+    half(10, 0)
     exchange(11, v, NX)
-    half(11, 1, True)
+    half(11, 1)
     exchange(12, v, NX)
 
-    @pl.loop(0, NX)
-    def _(x):
-        c, nb = fine_nb(12, x)
-        sol_out[x] = c[:, :NZ]
-        res_out[x] = (rh[x] - (dg[x] * c - nb))[:, :NZ]
+    def finish(xs, hoods):
+        for x, hood in zip(xs, hoods):
+            c, nb = fine_nb(x, hood)
+            sol_out[x] = c[:, :NZ]
+            res_out[x] = (rh[x] - (dg[x] * c - nb))[:, :NZ]
+
+    level_pass(NX, 1, finish, staged=False, field=v, e=12)
 
     @pl.loop(1, members)
     def _(k):
@@ -417,9 +447,9 @@
                 coarse, coarse, coarse, coarse,
                 pltpu.VMEM((EXCHANGES, 2, NY, LANES), F32),
                 pltpu.VMEM((EXCHANGES, 2, NX, LANES), F32),
-                pltpu.VMEM((EXCHANGES, 2, NY, LANES), F32),
+                pltpu.VMEM((EXCHANGES, 2, 2, NY, LANES), F32),
                 pltpu.VMEM((2, NX, LANES), F32),
-                pltpu.VMEM((NY, LANES), F32),
+                pltpu.VMEM((2, NY, LANES), F32),
                 dma((members,)), dma((members,)),
                 dma((3, members)), dma((3, members)),
                 dma((3, members)), dma((3, members)),

time: 261 us -> 166 us (0.64)
  Pallas kernels: 254 us -> 160 us
    pallas_call x1, Pallas kernels: 254 us -> 160 us  [body(): pl.pallas_call(functools.partial(kernel, sizes), out_shape=[jax.ShapeDtyp...]
where the time goes in v2:
time: 166 us
  Pallas kernels  160 us (96%)
  local copies, waits for them, and re-layouts  5.87 us (4%)
    pallas_call x1, Pallas kernels, body(): pl.pallas_call(functools.partial(kernel, sizes), out_shape=[jax.ShapeDtyp...  160 us
    unnamed x10, local copies, waits for them, and re-layouts  5.71 us

profile of v2, /device:TPU:0, one launch (start us, length us, event | category | flops | bytes accessed | tf_op | source)
XLA Modules:
  0.0 166.1 jit_solution(7552685216645469550)
XLA Ops:
  0.6 0.0 copy-start.3
  0.6 0.6 copy-done.3
  1.3 0.1 broadcast_in_dim_tile.3
  1.4 0.1 broadcast_in_dim.11.place_ref
  1.5 0.0 copy-start
  1.5 1.0 copy-done
  2.5 0.0 copy-start.1
  2.5 1.0 copy-done.1
  3.5 0.0 copy-start.2
  3.5 1.0 copy-done.2
  4.6 159.6 %shard_map.59 = (f32[64,32,64]{2,1,0:T(8,128)S(1)}, f32[64,32,64]{2,1,0:T(8,128)S(1)}) custom-call(s32[8,128]{1,0:T(8,128)S(1)} %broadcast_in_dim.11.place_ref, f32[1024,128]{1,0:T(8,128)S(1)} %bitcast.16, f32[1024,128]{1,0:T(8,128)S(1)} %bitcast.17, f32[1024,128]{1,0:T(8,128)S(1)} %bitcast.18), custom_call_target="tpu_custom_call" | custom-call | tf_op jit(solution)/shard_map/pallas_call | solution.py:429
  164.2 1.0 copy.11
  165.2 1.0 copy.12
  (2 shorter events, 0.0 us)
Async XLA Ops:
  0.6 0.7 copy-start.3
  1.5 1.0 copy-start
  2.5 1.0 copy-start.1
  3.5 1.0 copy-start.2

commit v3 on v2

--- a/solution.py
+++ b/solution.py
@@ -9,6 +9,7 @@
 
 MESH = pl.DeviceIdType.MESH
 NX, NY, NZ = 64, 32, 64
+PLANES = NX // 2
 LANES = 128
 COARSE_HALVES = 8
 EXCHANGES = 13
@@ -73,8 +74,8 @@
     def _(e):
         for side in range(2):
             hx[e, side] = jnp.zeros((NY, LANES), F32)
-            hy[e, side] = jnp.zeros((NX, LANES), F32)
-            hz[e, side] = jnp.zeros((2, NY, LANES), F32)
+            hy[e, side] = jnp.zeros((PLANES, LANES), F32)
+            hz[e, side] = jnp.zeros((NY, LANES), F32)
 
     barrier = pltpu.get_barrier_semaphore()
 
@@ -174,16 +175,15 @@
 
         @pl.loop(0, members)
         def _(j):
-            for qx in range(2):
-                for slab in range(slabs):
-                    low = qx * 2 * rows + slab * 8
-                    t0 = final[f, j, low:low + 8, :]
-                    t1 = final[f, j, low + rows:low + rows + 8, :]
-                    x = qx * 32 + j * slabs + slab
-                    for yr in range(4):
-                        r0 = pltpu.roll(t0, (LANES - 32 * yr) % LANES, 1)
-                        r1 = pltpu.roll(t1, (LANES + 32 - 32 * yr) % LANES, 1)
-                        out[x + first, pl.ds(yr, 8, stride=4), :] = jnp.where(lane8 < 32, r0, r1)
+            for slab in range(slabs):
+                tiles = [final[f, j, q * rows + slab * 8:q * rows + slab * 8 + 8, :] for q in range(4)]
+                for yr in range(4):
+                    whole = tiles[yr]
+                    for q in range(4):
+                        if q != yr:
+                            turned = pltpu.roll(tiles[q], (32 * (q - yr)) % LANES, 1)
+                            whole = jnp.where(lane8 // 32 == q, turned, whole)
+                    out[j * slabs + slab + first, pl.ds(yr, 8, stride=4), :] = whole
 
     def exchange(e, field, planes):
         for act in ("start", "wait"):
@@ -219,53 +219,43 @@
                                 recv_sem=halo_recv.at[e, d],
                                 device_id=tuple(other), device_id_type=MESH,
                             ).wait_recv()
-        field[0] = hx[e, 0]
-        field[planes + 1] = hx[e, 1]
+        low, lane = field[1], lane_ids()
+        field[0] = pltpu.roll(jnp.where(lane >= NZ, hx[e, 0], field[planes]), NZ, 1)
+        field[planes + 1] = pltpu.roll(jnp.where(lane < NZ, hx[e, 1], low), NZ, 1)
 
     def level_pass(planes, st, body, staged=True, field=None, e=None):
-        half_planes = planes // 2
-        spot = ((lane_ids() + st) % LANES) // st
         lane, row = lane_ids(), row_ids()
-        for h in range(2):
+        spot = ((lane + st) % NZ) // (2 * st)
+        if e is not None:
+            beyond = jnp.where((lane // st) % 2 == 0, hz[e, 1], pltpu.roll(hz[e, 0], 2 * st, 1))
+
+        def step(g, packed):
+            xs = [g * GROUP + i for i in range(GROUP)]
+            hoods = [None] * GROUP
             if e is not None:
-                beyond = jnp.where(spot < 48 // st, hz[e, 0, h], hz[e, 1, h])
-
-            def step(g, packed):
-                near = [g * GROUP + i for i in range(GROUP)]
-                xs = [h * half_planes + n for n in near]
-                hoods = [None] * GROUP
-                if e is not None:
-                    loaded = [field[xs[0] + i] for i in range(GROUP + 2)]
-                    hoods = []
-                    for i in range(GROUP):
-                        c = loaded[i + 1]
-                        yl = jnp.where(row < st, hy[e, 0, pl.ds(xs[i], 1), :], pltpu.roll(c, st, 0))
-                        yh = jnp.where(
-                            row >= NY - st, hy[e, 1, pl.ds(xs[i], 1), :], pltpu.roll(c, NY - st, 0)
-                        )
-                        w = jnp.where(
-                            lane >= NZ, pltpu.roll(beyond, (LANES - near[i] * st) % LANES, 1), c
-                        )
-                        zl, zh = pltpu.roll(w, st, 1), pltpu.roll(w, LANES - st, 1)
-                        hoods.append((c, loaded[i], loaded[i + 2], yl, yh, zl, zh))
-                results = body(xs, hoods)
-                if staged:
-                    for i in range(GROUP):
-                        n = results[i]
-                        turned = pltpu.roll(n, (near[i] * st + 64) % LANES, 1)
-                        mine = (spot == near[i]) | (spot == near[i] + 64 // st + 1)
-                        packed = jnp.where(mine, turned, packed)
-                    for i in range(GROUP):
-                        ys[0, pl.ds(xs[i], 1), :] = results[i][0:1, :]
-                        ys[1, pl.ds(xs[i], 1), :] = results[i][NY - 1:NY, :]
-                    return packed
-                return packed
-
-            steps = half_planes // GROUP
+                loaded = [field[xs[0] + i] for i in range(GROUP + 2)]
+                hoods = []
+                for i in range(GROUP):
+                    c = loaded[i + 1]
+                    yl = jnp.where(row < st, hy[e, 0, pl.ds(xs[i], 1), :], pltpu.roll(c, st, 0))
+                    yh = jnp.where(row >= NY - st, hy[e, 1, pl.ds(xs[i], 1), :], pltpu.roll(c, NY - st, 0))
+                    w = pltpu.roll(beyond, (LANES + NZ - st - xs[i] * (2 * st)) % LANES, 1)
+                    zl = jnp.where(lane % NZ < st, w, pltpu.roll(c, st, 1))
+                    zh = jnp.where(lane % NZ >= NZ - st, w, pltpu.roll(c, LANES - st, 1))
+                    hoods.append((c, loaded[i], loaded[i + 2], yl, yh, zl, zh))
+            results = body(xs, hoods)
             if staged:
-                zs[h] = lax.fori_loop(0, steps, step, jnp.zeros((NY, LANES), F32))
-            else:
-                lax.fori_loop(0, steps, step, 0)
+                for x, n in zip(xs, results):
+                    packed = jnp.where(spot == x, pltpu.roll(n, x * (2 * st), 1), packed)
+                for x, n in zip(xs, results):
+                    ys[0, pl.ds(x, 1), :] = n[0:1, :]
+                    ys[1, pl.ds(x, 1), :] = n[NY - 1:NY, :]
+            return packed
+
+        if staged:
+            zs[...] = lax.fori_loop(0, planes // GROUP, step, jnp.zeros((NY, LANES), F32))
+        else:
+            lax.fori_loop(0, planes // GROUP, step, 0)
 
     def fine_nb(x, hood):
         c, xl, xh, yl, yh, zl, zh = hood
@@ -285,8 +275,8 @@
     forward(0)
     forward(1)
     unpack(0, bv, 1)
-    level_pass(NX, 1, lambda xs, hoods: [bv[x + 1] for x in xs])
-    exchange(0, bv, NX)
+    level_pass(PLANES, 1, lambda xs, hoods: [bv[x + 1] for x in xs])
+    exchange(0, bv, PLANES)
     forward(2)
 
     def faces(xs, hoods):
@@ -297,12 +287,12 @@
             fzl[x] = 0.5 * (c + zl)
             fzh[x] = 0.5 * (c + zh)
 
-    level_pass(NX, 1, faces, staged=False, field=bv, e=0)
-    fx[NX] = 0.5 * (bv[NX] + bv[NX + 1])
+    level_pass(PLANES, 1, faces, staged=False, field=bv, e=0)
+    fx[PLANES] = 0.5 * (bv[PLANES] + bv[PLANES + 1])
 
     unpack(1, ac, 0)
 
-    @pl.loop(0, NX // 2)
+    @pl.loop(0, PLANES // 2)
     def _(i):
         x = 2 * i
         for o in range(2):
@@ -345,12 +335,12 @@
                 values.append(jnp.where(is_colour(x, 1, colour), (rh[x] + nb) * rd[x], c))
             return store(v, xs, values)
 
-        level_pass(NX, 1, update, field=v, e=e)
-
-    level_pass(NX, 1, first_red)
-    exchange(1, v, NX)
+        level_pass(PLANES, 1, update, field=v, e=e)
+
+    level_pass(PLANES, 1, first_red)
+    exchange(1, v, PLANES)
     half(1, 1)
-    exchange(2, v, NX)
+    exchange(2, v, PLANES)
 
     def restrict(xs, hoods):
         for p in range(0, GROUP, 2):
@@ -361,17 +351,17 @@
                 total = r if total is None else total + r
             cf[xs[p] // 2] = 0.125 * pair_z(pair_y(total))
 
-    level_pass(NX, 1, restrict, staged=False, field=v, e=2)
+    level_pass(PLANES, 1, restrict, staged=False, field=v, e=2)
 
     def first_coarse(xs, hoods):
         return store(cc, xs, [jnp.where(is_colour(x, 2, 0), cf[x] * crd[x], 0.0) for x in xs])
 
-    level_pass(NX // 2, 2, first_coarse)
+    level_pass(PLANES // 2, 2, first_coarse)
 
     @pl.loop(1, COARSE_HALVES)
     def _(h):
         e = 2 + h
-        exchange(e, cc, NX // 2)
+        exchange(e, cc, PLANES // 2)
 
         def update(xs, hoods):
             values = []
@@ -380,26 +370,28 @@
                 values.append(jnp.where(is_colour(x, 2, h), (cf[x] + nb) * crd[x], c))
             return store(cc, xs, values)
 
-        level_pass(NX // 2, 2, update, field=cc, e=e)
+        level_pass(PLANES // 2, 2, update, field=cc, e=e)
 
     def correct(xs, hoods):
         coarse = [cc[xs[p] // 2 + 1] for p in range(0, GROUP, 2)]
         return store(v, xs, [v[x + 1] + coarse[i // 2] for i, x in enumerate(xs)])
 
-    level_pass(NX, 1, correct)
-    exchange(10, v, NX)
+    level_pass(PLANES, 1, correct)
+    exchange(10, v, PLANES)
     half(10, 0)
-    exchange(11, v, NX)
+    exchange(11, v, PLANES)
     half(11, 1)
-    exchange(12, v, NX)
+    exchange(12, v, PLANES)
 
     def finish(xs, hoods):
         for x, hood in zip(xs, hoods):
             c, nb = fine_nb(x, hood)
-            sol_out[x] = c[:, :NZ]
-            res_out[x] = (rh[x] - (dg[x] * c - nb))[:, :NZ]
-
-    level_pass(NX, 1, finish, staged=False, field=v, e=12)
+            r = rh[x] - (dg[x] * c - nb)
+            for out, n in ((sol_out, c), (res_out, r)):
+                out[x] = n[:, :NZ]
+                out[x + PLANES] = pltpu.roll(n, NZ, 1)[:, :NZ]
+
+    level_pass(PLANES, 1, finish, staged=False, field=v, e=12)
 
     @pl.loop(1, members)
     def _(k):
@@ -421,8 +413,8 @@
     def body(rhs_boxes, a_boxes, b_boxes, new_place):
         spot = jnp.where(jnp.arange(8)[:, None] < 4, jnp.tile(new_place[0], 2)[:, None], -1)
         spot = jnp.broadcast_to(spot, (8, LANES)).astype(jnp.int32)
-        fine = pltpu.VMEM((NX, NY, LANES), F32)
-        coarse = pltpu.VMEM((NX // 2, NY, LANES), F32)
+        fine = pltpu.VMEM((PLANES, NY, LANES), F32)
+        coarse = pltpu.VMEM((PLANES // 2, NY, LANES), F32)
         box = pltpu.VMEM((members, 4 * rows, LANES), F32)
         boxes = pltpu.VMEM((3, members, 4 * rows, LANES), F32)
         dma = pltpu.SemaphoreType.DMA
@@ -436,20 +428,20 @@
                 pltpu.VMEM((8, LANES), jnp.int32),
                 pltpu.SMEM((8, LANES), jnp.int32),
                 box, box, box, boxes, boxes,
-                pltpu.VMEM((NX + 2, NY, LANES), F32),
+                pltpu.VMEM((PLANES + 2, NY, LANES), F32),
                 fine, fine, fine, fine,
-                pltpu.VMEM((NX + 1, NY, LANES), F32),
+                pltpu.VMEM((PLANES + 1, NY, LANES), F32),
                 fine, fine, fine, fine,
-                pltpu.VMEM((NX + 2, NY, LANES), F32),
-                pltpu.VMEM((NX // 2 + 2, NY, LANES), F32),
+                pltpu.VMEM((PLANES + 2, NY, LANES), F32),
+                pltpu.VMEM((PLANES // 2 + 2, NY, LANES), F32),
                 coarse, coarse,
-                pltpu.VMEM((NX // 2 + 1, NY, LANES), F32),
+                pltpu.VMEM((PLANES // 2 + 1, NY, LANES), F32),
                 coarse, coarse, coarse, coarse,
                 pltpu.VMEM((EXCHANGES, 2, NY, LANES), F32),
-                pltpu.VMEM((EXCHANGES, 2, NX, LANES), F32),
-                pltpu.VMEM((EXCHANGES, 2, 2, NY, LANES), F32),
-                pltpu.VMEM((2, NX, LANES), F32),
-                pltpu.VMEM((2, NY, LANES), F32),
+                pltpu.VMEM((EXCHANGES, 2, PLANES, LANES), F32),
+                pltpu.VMEM((EXCHANGES, 2, NY, LANES), F32),
+                pltpu.VMEM((2, PLANES, LANES), F32),
+                pltpu.VMEM((NY, LANES), F32),
                 dma((members,)), dma((members,)),
                 dma((3, members)), dma((3, members)),
                 dma((3, members)), dma((3, members)),

time: 166 us -> 144 us (0.87)
  Pallas kernels: 160 us -> 137 us
    pallas_call x1, Pallas kernels: 160 us -> 137 us  [body(): pl.pallas_call(functools.partial(kernel, sizes), out_shape=[jax.ShapeDtyp...]
where the time goes in v3:
time: 144 us
  Pallas kernels  137 us (95%)
  local copies, waits for them, and re-layouts  5.87 us (4%)
    pallas_call x1, Pallas kernels, body(): pl.pallas_call(functools.partial(kernel, sizes), out_shape=[jax.ShapeDtyp...  137 us
    unnamed x10, local copies, waits for them, and re-layouts  5.71 us

profile of v3, /device:TPU:0, one launch (start us, length us, event | category | flops | bytes accessed | tf_op | source)
XLA Modules:
  0.0 143.6 jit_solution(7650275639360429665)
XLA Ops:
  0.6 0.0 copy-start.3
  0.6 0.6 copy-done.3
  1.3 0.1 broadcast_in_dim_tile.3
  1.4 0.1 broadcast_in_dim.11.place_ref
  1.5 0.0 copy-start
  1.5 1.0 copy-done
  2.5 0.0 copy-start.1
  2.5 1.0 copy-done.1
  3.5 0.0 copy-start.2
  3.5 1.0 copy-done.2
  4.6 137.1 %shard_map.59 = (f32[64,32,64]{2,1,0:T(8,128)S(1)}, f32[64,32,64]{2,1,0:T(8,128)S(1)}) custom-call(s32[8,128]{1,0:T(8,128)S(1)} %broadcast_in_dim.11.place_ref, f32[1024,128]{1,0:T(8,128)S(1)} %bitcast.16, f32[1024,128]{1,0:T(8,128)S(1)} %bitcast.17, f32[1024,128]{1,0:T(8,128)S(1)} %bitcast.18), custom_call_target="tpu_custom_call" | custom-call | tf_op jit(solution)/shard_map/pallas_call | solution.py:421
  141.7 1.0 copy.11
  142.7 1.0 copy.12
  (2 shorter events, 0.0 us)
Async XLA Ops:
  0.6 0.7 copy-start.3
  1.5 1.0 copy-start
  2.5 1.0 copy-start.1
  3.5 1.0 copy-start.2

commit v4 on v3

--- a/solution.py
+++ b/solution.py
@@ -121,14 +121,22 @@
     def _(k):
         place_copy((me + k) % members, k, me).start()
 
-    for f in range(3):
+    def own1(f):
+        return pltpu.make_async_copy(
+            (b_in, a_in, rhs_in)[f].at[pl.ds(pl.multiple_of(me * 4 * rows, 8), 4 * rows)],
+            got[f].at[me], recv1.at[f, me],
+        )
+
+    def send_pieces(f):
+        own1(f).start()
+
         @pl.loop(1, members)
         def _(k):
             copy1(f, (me + k) % members, k, me).start()
 
+    send_pieces(0)
+    send_pieces(1)
     got_place[me] = place_ref[...]
-    for f in range(3):
-        got[f][me] = (b_in, a_in, rhs_in)[f][pl.ds(pl.multiple_of(me * 4 * rows, 8), 4 * rows), :]
 
     @pl.loop(1, members)
     def _(k):
@@ -150,6 +158,8 @@
     inv_copy.wait()
 
     def forward(f):
+        own1(f).wait()
+
         @pl.loop(1, members)
         def _(k):
             copy1(f, (me + k) % members, k, (me + k) % members).wait_recv()
@@ -185,8 +195,8 @@
                             whole = jnp.where(lane8 // 32 == q, turned, whole)
                     out[j * slabs + slab + first, pl.ds(yr, 8, stride=4), :] = whole
 
-    def exchange(e, field, planes):
-        for act in ("start", "wait"):
+    def exchange(e, field, planes, acts=("start", "wait")):
+        for act in acts:
             for axis in range(3):
                 for side in range(2):
                     d = axis * 2 + side
@@ -219,6 +229,8 @@
                                 recv_sem=halo_recv.at[e, d],
                                 device_id=tuple(other), device_id_type=MESH,
                             ).wait_recv()
+        if "wait" not in acts:
+            return
         low, lane = field[1], lane_ids()
         field[0] = pltpu.roll(jnp.where(lane >= NZ, hx[e, 0], field[planes]), NZ, 1)
         field[planes + 1] = pltpu.roll(jnp.where(lane < NZ, hx[e, 1], low), NZ, 1)
@@ -273,11 +285,13 @@
         return (row_ids() // st + lane_ids() // st + x + colour) % 2 == 0
 
     forward(0)
+    send_pieces(2)
     forward(1)
     unpack(0, bv, 1)
     level_pass(PLANES, 1, lambda xs, hoods: [bv[x + 1] for x in xs])
-    exchange(0, bv, PLANES)
+    exchange(0, bv, PLANES, ("start",))
     forward(2)
+    exchange(0, bv, PLANES, ("wait",))
 
     def faces(xs, hoods):
         for x, (c, xl, xh, yl, yh, zl, zh) in zip(xs, hoods):
@@ -421,7 +435,7 @@
         return pl.pallas_call(
             functools.partial(kernel, sizes),
             out_shape=[jax.ShapeDtypeStruct((NX, NY, NZ), F32)] * 2,
-            in_specs=[pl.BlockSpec(memory_space=pltpu.VMEM)] * 4,
+            in_specs=[pl.BlockSpec(memory_space=pltpu.VMEM)] + [pl.BlockSpec(memory_space=pltpu.HBM)] * 3,
             out_specs=[pl.BlockSpec(memory_space=pltpu.VMEM)] * 2,
             scratch_shapes=[
                 pltpu.VMEM((members, 8, LANES), jnp.int32),

time: 144 us -> 143 us (level)
  no operation moved by 1% of the time
where the time goes in v4:
time: 143 us; the launch traced here: 142 us
  Pallas kernels  136 us (95%)
  local copies, waits for them, and re-layouts  5.87 us (4%)
    pallas_call x1, Pallas kernels, body(): pl.pallas_call(functools.partial(kernel, sizes), out_shape=[jax.ShapeDtyp...  136 us
    unnamed x10, local copies, waits for them, and re-layouts  5.71 us

profile of v4, /device:TPU:0, one launch (start us, length us, event | category | flops | bytes accessed | tf_op | source)
XLA Modules:
  0.0 142.2 jit_solution(16222333456301604840)
XLA Ops:
  0.6 0.0 copy-start.3
  0.6 0.6 copy-done.3
  1.3 0.1 broadcast_in_dim_tile.3
  1.4 0.1 broadcast_in_dim.11.place_ref
  1.5 0.0 copy-start
  1.5 1.0 copy-done
  2.5 0.0 copy-start.1
  2.5 1.0 copy-done.1
  3.5 0.0 copy-start.2
  3.5 1.0 copy-done.2
  4.6 135.7 %shard_map.59 = (f32[64,32,64]{2,1,0:T(8,128)S(1)}, f32[64,32,64]{2,1,0:T(8,128)S(1)}) custom-call(s32[8,128]{1,0:T(8,128)S(1)} %broadcast_in_dim.11.place_ref, f32[1024,128]{1,0:T(8,128)S(1)} %bitcast.16, f32[1024,128]{1,0:T(8,128)S(1)} %bitcast.17, f32[1024,128]{1,0:T(8,128)S(1)} %bitcast.18), custom_call_target="tpu_custom_call" | custom-call | tf_op jit(solution)/shard_map/pallas_call | solution.py:435
  140.3 1.0 copy.11
  141.3 1.0 copy.12
  (2 shorter events, 0.0 us)
Async XLA Ops:
  0.6 0.7 copy-start.3
  1.5 1.0 copy-start
  2.5 1.0 copy-start.1
  3.5 1.0 copy-start.2

commit v5 on v4

--- a/solution.py
+++ b/solution.py
@@ -13,7 +13,7 @@
 LANES = 128
 COARSE_HALVES = 8
 EXCHANGES = 13
-GROUP = 4
+GROUP = 8
 F32 = jnp.float32
 
 
@@ -197,7 +197,7 @@
 
     def exchange(e, field, planes, acts=("start", "wait")):
         for act in acts:
-            for axis in range(3):
+            for axis in (1, 0, 2):
                 for side in range(2):
                     d = axis * 2 + side
                     place, count = ((gx, n_gx), (gy, n_gy), (gz, n_gz))[axis]
@@ -463,7 +463,7 @@
                 dma((6,)), dma((EXCHANGES, 6)),
             ],
             compiler_params=pltpu.CompilerParams(
-                collective_id=0, has_side_effects=True, vmem_limit_bytes=48 * 1024 * 1024
+                collective_id=0, has_side_effects=True, vmem_limit_bytes=60 * 1024 * 1024
             ),
         )(spot, rows128(rhs_boxes), rows128(a_boxes), rows128(b_boxes))
 

time: 143 us -> 138 us (0.965)
  Pallas kernels: 136 us -> 132 us
    pallas_call x1, Pallas kernels: 136 us -> 132 us  [body(): pl.pallas_call(functools.partial(kernel, sizes), out_shape=[jax.ShapeDtyp...]
    unnamed x10 -> x6, local copies, waits for them, and re-layouts: 5.71 us -> 3.97 us
where the time goes in v5:
time: 138 us
  Pallas kernels  132 us (96%)
  local copies, waits for them, and re-layouts  4.72 us (3%)
    pallas_call x1, Pallas kernels, body(): pl.pallas_call(functools.partial(kernel, sizes), out_shape=[jax.ShapeDtyp...  132 us
    unnamed x6, local copies, waits for them, and re-layouts  3.97 us

profile of v5, /device:TPU:0, one launch (start us, length us, event | category | flops | bytes accessed | tf_op | source)
XLA Modules:
  0.0 137.8 jit_solution(719947158675899252)
XLA Ops:
  0.6 0.0 copy-start.1
  0.6 0.6 copy-done.1
  1.3 0.1 broadcast_in_dim_tile.3
  1.4 0.7 broadcast_in_dim.11.place_ref
  2.0 132.4 %shard_map.59 = (f32[64,32,64]{2,1,0:T(8,128)}, f32[64,32,64]{2,1,0:T(8,128)}) custom-call(s32[8,128]{1,0:T(8,128)} %broadcast_in_dim.11.place_ref, f32[1024,128]{1,0:T(8,128)} %bitcast.16, f32[1024,128]{1,0:T(8,128)} %bitcast.17, f32[1024,128]{1,0:T(8,128)} %bitcast.18), custom_call_target="tpu_custom_call" | custom-call | tf_op jit(solution)/shard_map/pallas_call | solution.py:435
  134.4 0.0 copy-start
  134.5 2.4 %copy.11 = f32[64,32,64]{2,1,0:T(8,128)} copy(f32[64,32,64]{2,1,0:T(8,128)} %get-tuple-element.4) | data formatting | bytes 1048576
  136.8 0.0 copy-done
  136.8 1.0 copy.12
  (2 shorter events, 0.0 us)
Async XLA Ops:
  0.6 0.7 copy-start.1
  134.4 2.4 %copy-start = (f32[64,32,64]{2,1,0:T(8,128)S(1)}, f32[64,32,64]{2,1,0:T(8,128)}, u32[]{:S(2)}) copy-start(f32[64,32,64]{2,1,0:T(8,128)} %get-tuple-element.5) | copy-start | bytes 1572868

commit v6 on v5

--- a/solution.py
+++ b/solution.py
@@ -67,6 +67,12 @@
     me = gx * n_gy + gy
     got = (got_b, got_a, got_rhs)
 
+    def partner(k):
+        return (me + 1 + (k + members // 2 - 2) % (members - 1)) % members
+
+    def sender(k):
+        return (me + members - 1 - (k + members // 2 - 2) % (members - 1)) % members
+
     def member(t):
         return (t // n_gy, t % n_gy, gz)
 
@@ -119,7 +125,7 @@
 
     @pl.loop(1, members)
     def _(k):
-        place_copy((me + k) % members, k, me).start()
+        place_copy(partner(k), k, me).start()
 
     def own1(f):
         return pltpu.make_async_copy(
@@ -132,7 +138,7 @@
 
         @pl.loop(1, members)
         def _(k):
-            copy1(f, (me + k) % members, k, me).start()
+            copy1(f, partner(k), k, me).start()
 
     send_pieces(0)
     send_pieces(1)
@@ -170,7 +176,7 @@
 
         @pl.loop(1, members)
         def _(k):
-            t = (me + k) % members
+            t = partner(k)
             for q in range(4):
                 sorted_[f, t, q * rows:(q + 1) * rows, :] = pick(t, q)
             copy2(f, t, k, me).start()
@@ -179,12 +185,7 @@
             final[f, me, q * rows:(q + 1) * rows, :] = pick(me, q)
 
     def unpack(f, out, first):
-        @pl.loop(1, members)
-        def _(k):
-            copy2(f, (me + k) % members, k, (me + k) % members).wait_recv()
-
-        @pl.loop(0, members)
-        def _(j):
+        def one(j):
             for slab in range(slabs):
                 tiles = [final[f, j, q * rows + slab * 8:q * rows + slab * 8 + 8, :] for q in range(4)]
                 for yr in range(4):
@@ -194,6 +195,14 @@
                             turned = pltpu.roll(tiles[q], (32 * (q - yr)) % LANES, 1)
                             whole = jnp.where(lane8 // 32 == q, turned, whole)
                     out[j * slabs + slab + first, pl.ds(yr, 8, stride=4), :] = whole
+
+        one(me)
+
+        @pl.loop(1, members)
+        def _(k):
+            j = sender(k)
+            copy2(f, j, k, j).wait_recv()
+            one(j)
 
     def exchange(e, field, planes, acts=("start", "wait")):
         for act in acts:
@@ -235,9 +244,10 @@
         field[0] = pltpu.roll(jnp.where(lane >= NZ, hx[e, 0], field[planes]), NZ, 1)
         field[planes + 1] = pltpu.roll(jnp.where(lane < NZ, hx[e, 1], low), NZ, 1)
 
-    def level_pass(planes, st, body, staged=True, field=None, e=None):
+    def level_pass(planes, st, body, staged=True, field=None, e=None, out_st=None):
         lane, row = lane_ids(), row_ids()
-        spot = ((lane + st) % NZ) // (2 * st)
+        out_st = st if out_st is None else out_st
+        spot = ((lane + out_st) % NZ) // (2 * out_st)
         if e is not None:
             beyond = jnp.where((lane // st) % 2 == 0, hz[e, 1], pltpu.roll(hz[e, 0], 2 * st, 1))
 
@@ -257,9 +267,10 @@
                     hoods.append((c, loaded[i], loaded[i + 2], yl, yh, zl, zh))
             results = body(xs, hoods)
             if staged:
-                for x, n in zip(xs, results):
-                    packed = jnp.where(spot == x, pltpu.roll(n, x * (2 * st), 1), packed)
-                for x, n in zip(xs, results):
+                places = [g * len(results) + i for i in range(len(results))]
+                for x, n in zip(places, results):
+                    packed = jnp.where(spot == x, pltpu.roll(n, x * (2 * out_st), 1), packed)
+                for x, n in zip(places, results):
                     ys[0, pl.ds(x, 1), :] = n[0:1, :]
                     ys[1, pl.ds(x, 1), :] = n[NY - 1:NY, :]
             return packed
@@ -357,40 +368,47 @@
     exchange(2, v, PLANES)
 
     def restrict(xs, hoods):
+        values = []
         for p in range(0, GROUP, 2):
             total = None
             for x, hood in zip(xs[p:p + 2], hoods[p:p + 2]):
                 c, nb = fine_nb(x, hood)
                 r = rh[x] - (dg[x] * c - nb)
                 total = r if total is None else total + r
-            cf[xs[p] // 2] = 0.125 * pair_z(pair_y(total))
-
-    level_pass(PLANES, 1, restrict, staged=False, field=v, e=2)
-
-    def first_coarse(xs, hoods):
-        return store(cc, xs, [jnp.where(is_colour(x, 2, 0), cf[x] * crd[x], 0.0) for x in xs])
-
-    level_pass(PLANES // 2, 2, first_coarse)
-
-    @pl.loop(1, COARSE_HALVES)
+            values.append(0.125 * pair_z(pair_y(total)))
+        places = [xs[0] // 2 + i for i in range(GROUP // 2)]
+        for i, f in zip(places, values):
+            cf[i] = f
+        return store(
+            cc, places,
+            [jnp.where(is_colour(i, 2, 0), f * crd[i], 0.0) for i, f in zip(places, values)],
+        )
+
+    level_pass(PLANES, 1, restrict, field=v, e=2, out_st=2)
+
+    def coarse_half(h, xs, hoods):
+        values = []
+        for x, hood in zip(xs, hoods):
+            c, nb = coarse_nb(x, hood)
+            values.append(jnp.where(is_colour(x, 2, h), (cf[x] + nb) * crd[x], c))
+        return values
+
+    @pl.loop(1, COARSE_HALVES - 1)
     def _(h):
-        e = 2 + h
-        exchange(e, cc, PLANES // 2)
-
-        def update(xs, hoods):
-            values = []
-            for x, hood in zip(xs, hoods):
-                c, nb = coarse_nb(x, hood)
-                values.append(jnp.where(is_colour(x, 2, h), (cf[x] + nb) * crd[x], c))
-            return store(cc, xs, values)
-
-        level_pass(PLANES // 2, 2, update, field=cc, e=e)
+        exchange(2 + h, cc, PLANES // 2)
+        level_pass(
+            PLANES // 2, 2, lambda xs, hoods: store(cc, xs, coarse_half(h, xs, hoods)),
+            field=cc, e=2 + h,
+        )
 
     def correct(xs, hoods):
-        coarse = [cc[xs[p] // 2 + 1] for p in range(0, GROUP, 2)]
-        return store(v, xs, [v[x + 1] + coarse[i // 2] for i, x in enumerate(xs)])
-
-    level_pass(PLANES, 1, correct)
+        values = []
+        for x, n in zip(xs, coarse_half(COARSE_HALVES - 1, xs, hoods)):
+            values += [v[2 * x + 1] + n, v[2 * x + 2] + n]
+        return store(v, [2 * xs[0] + i for i in range(2 * GROUP)], values)
+
+    exchange(9, cc, PLANES // 2)
+    level_pass(PLANES // 2, 2, correct, field=cc, e=9, out_st=1)
     exchange(10, v, PLANES)
     half(10, 0)
     exchange(11, v, PLANES)
@@ -409,7 +427,7 @@
 
     @pl.loop(1, members)
     def _(k):
-        peer = (me + k) % members
+        peer = partner(k)
         place_copy(peer, k, me).wait_send()
         for f in range(3):
             copy1(f, peer, k, me).wait_send()

time: 138 us -> 137 us (level)
  no operation moved by 1% of the time
where the time goes in v6:
time: 137 us
  Pallas kernels  131 us (96%)
  local copies, waits for them, and re-layouts  4.72 us (3%)
    pallas_call x1, Pallas kernels, body(): pl.pallas_call(functools.partial(kernel, sizes), out_shape=[jax.ShapeDtyp...  131 us
    unnamed x6, local copies, waits for them, and re-layouts  3.97 us

profile of v6, /device:TPU:0, one launch (start us, length us, event | category | flops | bytes accessed | tf_op | source)
XLA Modules:
  0.0 136.7 jit_solution(10399538210010799127)
XLA Ops:
  0.6 0.0 copy-start.1
  0.6 0.6 copy-done.1
  1.3 0.1 broadcast_in_dim_tile.3
  1.4 0.7 broadcast_in_dim.11.place_ref
  2.0 131.3 %shard_map.59 = (f32[64,32,64]{2,1,0:T(8,128)}, f32[64,32,64]{2,1,0:T(8,128)}) custom-call(s32[8,128]{1,0:T(8,128)} %broadcast_in_dim.11.place_ref, f32[1024,128]{1,0:T(8,128)} %bitcast.16, f32[1024,128]{1,0:T(8,128)} %bitcast.17, f32[1024,128]{1,0:T(8,128)} %bitcast.18), custom_call_target="tpu_custom_call" | custom-call | tf_op jit(solution)/shard_map/pallas_call | solution.py:453
  133.3 0.0 copy-start
  133.3 2.4 %copy.11 = f32[64,32,64]{2,1,0:T(8,128)} copy(f32[64,32,64]{2,1,0:T(8,128)} %get-tuple-element.4) | data formatting | bytes 1048576
  135.7 0.0 copy-done
  135.7 1.0 copy.12
  (2 shorter events, 0.0 us)
Async XLA Ops:
  0.6 0.7 copy-start.1
  133.3 2.4 %copy-start = (f32[64,32,64]{2,1,0:T(8,128)S(1)}, f32[64,32,64]{2,1,0:T(8,128)}, u32[]{:S(2)}) copy-start(f32[64,32,64]{2,1,0:T(8,128)} %get-tuple-element.5) | copy-start | bytes 1572868

commit v7 on v6

--- a/solution.py
+++ b/solution.py
@@ -56,6 +56,7 @@
     got_place, inv_vmem, inv_smem, got_b, got_a, got_rhs, sorted_, final,
     bv, rh, ac, dg, rd, fx, fyl, fyh, fzl, fzh, v,
     cc, cf, crd, cfx, cfyl, cfyh, cfzl, cfzh,
+    fye, fze, cfye, cfze, inner,
     hx, hy, hz, ys, zs,
     place_send, place_recv, send1, recv1, send2, recv2, inv_sem, halo_send, halo_recv,
 ):
@@ -206,6 +207,8 @@
 
     def exchange(e, field, planes, acts=("start", "wait")):
         for act in acts:
+            if act == "only":
+                continue
             for axis in (1, 0, 2):
                 for side in range(2):
                     d = axis * 2 + side
@@ -238,7 +241,7 @@
                                 recv_sem=halo_recv.at[e, d],
                                 device_id=tuple(other), device_id_type=MESH,
                             ).wait_recv()
-        if "wait" not in acts:
+        if acts[-1] != "wait":
             return
         low, lane = field[1], lane_ids()
         field[0] = pltpu.roll(jnp.where(lane >= NZ, hx[e, 0], field[planes]), NZ, 1)
@@ -280,17 +283,57 @@
         else:
             lax.fori_loop(0, planes // GROUP, step, 0)
 
-    def fine_nb(x, hood):
-        c, xl, xh, yl, yh, zl, zh = hood
-        return c, (
-            (fx[x] * xl + fx[x + 1] * xh) + (fyl[x] * yl + fyh[x] * yh) + (fzl[x] * zl + fzh[x] * zh)
-        )
-
-    def coarse_nb(x, hood):
-        c, xl, xh, yl, yh, zl, zh = hood
-        return c, (
-            (cfx[x] * xl + cfx[x + 1] * xh) + (cfyl[x] * yl + cfyh[x] * yh) + (cfzl[x] * zl + cfzh[x] * zh)
-        )
+    fine_faces = (fx, fyl, fyh, fzl, fzh, fye, fze)
+    coarse_faces = (cfx, cfyl, cfyh, cfzl, cfzh, cfye, cfze)
+
+    def split_faces(st, yl, yh, zl, zh):
+        row, z = row_ids(), lane_ids() % NZ
+        y_low, y_high, z_low, z_high = row < st, row >= NY - st, z < st, z >= NZ - st
+        return (
+            jnp.where(y_low, 0.0, yl), jnp.where(y_high, 0.0, yh),
+            jnp.where(z_low, 0.0, zl), jnp.where(z_high, 0.0, zh),
+            jnp.where(y_low, yl, jnp.where(y_high, yh, 0.0)),
+            jnp.where(z_low, zl, jnp.where(z_high, zh, 0.0)),
+        )
+
+    def halo_pass(field, e, planes, st, faces, body, staged=True, out_st=None):
+        across, yl, yh, zl, zh, ye, ze = faces
+        exchange(e, field, planes, ("start",))
+        lane = lane_ids()
+        first, last = field[1], field[planes]
+        field[0] = pltpu.roll(jnp.where(lane < NZ, last, 0.0), NZ, 1)
+        field[planes + 1] = pltpu.roll(jnp.where(lane >= NZ, first, 0.0), NZ, 1)
+
+        @pl.loop(0, planes // GROUP)
+        def _(g):
+            xs = [g * GROUP + i for i in range(GROUP)]
+            loaded = [field[xs[0] + i] for i in range(GROUP + 2)]
+            sums = []
+            for i, x in enumerate(xs):
+                c = loaded[i + 1]
+                sums.append(
+                    (across[x] * loaded[i] + across[x + 1] * loaded[i + 2])
+                    + (yl[x] * pltpu.roll(c, st, 0) + yh[x] * pltpu.roll(c, NY - st, 0))
+                    + (zl[x] * pltpu.roll(c, st, 1) + zh[x] * pltpu.roll(c, LANES - st, 1))
+                )
+            for x, total in zip(xs, sums):
+                inner[x] = total
+
+        exchange(e, field, planes, ("wait", "only"))
+        inner[0] += across[0] * pltpu.roll(jnp.where(lane >= NZ, hx[e, 0], 0.0), NZ, 1)
+        inner[planes - 1] += across[planes] * pltpu.roll(jnp.where(lane < NZ, hx[e, 1], 0.0), NZ, 1)
+        beyond = jnp.where((lane // st) % 2 == 0, hz[e, 1], pltpu.roll(hz[e, 0], 2 * st, 1))
+        lower = row_ids() < NY // 2
+
+        def with_halos(xs, hoods):
+            pairs = []
+            for x in xs:
+                w = pltpu.roll(beyond, (LANES + NZ - st - x * (2 * st)) % LANES, 1)
+                y = jnp.where(lower, hy[e, 0, pl.ds(x, 1), :], hy[e, 1, pl.ds(x, 1), :])
+                pairs.append((field[x + 1], inner[x] + (ye[x] * y + ze[x] * w)))
+            return body(xs, pairs)
+
+        level_pass(planes, st, with_halos, staged=staged, out_st=out_st)
 
     def is_colour(x, st, colour):
         return (row_ids() // st + lane_ids() // st + x + colour) % 2 == 0
@@ -335,12 +378,14 @@
         wzh = s * pair_y(odd_z(fzh[x] + fzh[x + 1]))
         cfx[i] = wxl
         cfx[i + 1] = wxh
-        cfyl[i] = wyl
-        cfyh[i] = wyh
-        cfzl[i] = wzl
-        cfzh[i] = wzh
+        for ref, face in zip(coarse_faces[1:], split_faces(2, wyl, wyh, wzl, wzh)):
+            ref[i] = face
         ca = 0.125 * pair_z(pair_y(ac[x] + ac[x + 1]))
         crd[i] = 1.0 / (ca + ((wxl + wxh) + (wyl + wyh) + (wzl + wzh)))
+        for o in range(2):
+            full = split_faces(1, fyl[x + o], fyh[x + o], fzl[x + o], fzh[x + o])
+            for ref, face in zip(fine_faces[1:], full):
+                ref[x + o] = face
 
     unpack(2, rh, 0)
 
@@ -356,23 +401,21 @@
         def update(xs, hoods):
             values = []
             for x, hood in zip(xs, hoods):
-                c, nb = fine_nb(x, hood)
+                c, nb = hood
                 values.append(jnp.where(is_colour(x, 1, colour), (rh[x] + nb) * rd[x], c))
             return store(v, xs, values)
 
-        level_pass(PLANES, 1, update, field=v, e=e)
+        halo_pass(v, e, PLANES, 1, fine_faces, update)
 
     level_pass(PLANES, 1, first_red)
-    exchange(1, v, PLANES)
     half(1, 1)
-    exchange(2, v, PLANES)
 
     def restrict(xs, hoods):
         values = []
         for p in range(0, GROUP, 2):
             total = None
             for x, hood in zip(xs[p:p + 2], hoods[p:p + 2]):
-                c, nb = fine_nb(x, hood)
+                c, nb = hood
                 r = rh[x] - (dg[x] * c - nb)
                 total = r if total is None else total + r
             values.append(0.125 * pair_z(pair_y(total)))
@@ -384,21 +427,20 @@
             [jnp.where(is_colour(i, 2, 0), f * crd[i], 0.0) for i, f in zip(places, values)],
         )
 
-    level_pass(PLANES, 1, restrict, field=v, e=2, out_st=2)
+    halo_pass(v, 2, PLANES, 1, fine_faces, restrict, out_st=2)
 
     def coarse_half(h, xs, hoods):
         values = []
         for x, hood in zip(xs, hoods):
-            c, nb = coarse_nb(x, hood)
+            c, nb = hood
             values.append(jnp.where(is_colour(x, 2, h), (cf[x] + nb) * crd[x], c))
         return values
 
     @pl.loop(1, COARSE_HALVES - 1)
     def _(h):
-        exchange(2 + h, cc, PLANES // 2)
-        level_pass(
-            PLANES // 2, 2, lambda xs, hoods: store(cc, xs, coarse_half(h, xs, hoods)),
-            field=cc, e=2 + h,
+        halo_pass(
+            cc, 2 + h, PLANES // 2, 2, coarse_faces,
+            lambda xs, hoods: store(cc, xs, coarse_half(h, xs, hoods)),
         )
 
     def correct(xs, hoods):
@@ -407,23 +449,19 @@
             values += [v[2 * x + 1] + n, v[2 * x + 2] + n]
         return store(v, [2 * xs[0] + i for i in range(2 * GROUP)], values)
 
-    exchange(9, cc, PLANES // 2)
-    level_pass(PLANES // 2, 2, correct, field=cc, e=9, out_st=1)
-    exchange(10, v, PLANES)
+    halo_pass(cc, 9, PLANES // 2, 2, coarse_faces, correct, out_st=1)
     half(10, 0)
-    exchange(11, v, PLANES)
     half(11, 1)
-    exchange(12, v, PLANES)
 
     def finish(xs, hoods):
         for x, hood in zip(xs, hoods):
-            c, nb = fine_nb(x, hood)
+            c, nb = hood
             r = rh[x] - (dg[x] * c - nb)
             for out, n in ((sol_out, c), (res_out, r)):
                 out[x] = n[:, :NZ]
                 out[x + PLANES] = pltpu.roll(n, NZ, 1)[:, :NZ]
 
-    level_pass(PLANES, 1, finish, staged=False, field=v, e=12)
+    halo_pass(v, 12, PLANES, 1, fine_faces, finish, staged=False)
 
     @pl.loop(1, members)
     def _(k):
@@ -469,6 +507,7 @@
                 coarse, coarse,
                 pltpu.VMEM((PLANES // 2 + 1, NY, LANES), F32),
                 coarse, coarse, coarse, coarse,
+                fine, fine, coarse, coarse, fine,
                 pltpu.VMEM((EXCHANGES, 2, NY, LANES), F32),
                 pltpu.VMEM((EXCHANGES, 2, PLANES, LANES), F32),
                 pltpu.VMEM((EXCHANGES, 2, NY, LANES), F32),

time: 137 us -> 135 us (0.985)
  Pallas kernels: 131 us -> 129 us
    pallas_call x1, Pallas kernels: 131 us -> 129 us  [body(): pl.pallas_call(functools.partial(kernel, sizes), out_shape=[jax.ShapeDtyp...]
where the time goes in v7:
time: 135 us; the launch traced here: 134 us
  Pallas kernels  129 us (96%)
  local copies, waits for them, and re-layouts  4.72 us (3%)
    pallas_call x1, Pallas kernels, body(): pl.pallas_call(functools.partial(kernel, sizes), out_shape=[jax.ShapeDtyp...  129 us
    unnamed x6, local copies, waits for them, and re-layouts  3.97 us

profile of v7, /device:TPU:0, one launch (start us, length us, event | category | flops | bytes accessed | tf_op | source)
XLA Modules:
  0.0 134.3 jit_solution(3294746841260601799)
XLA Ops:
  0.6 0.0 copy-start.1
  0.6 0.6 copy-done.1
  1.3 0.1 broadcast_in_dim_tile.3
  1.4 0.7 broadcast_in_dim.11.place_ref
  2.0 129.0 %shard_map.59 = (f32[64,32,64]{2,1,0:T(8,128)}, f32[64,32,64]{2,1,0:T(8,128)}) custom-call(s32[8,128]{1,0:T(8,128)} %broadcast_in_dim.11.place_ref, f32[1024,128]{1,0:T(8,128)} %bitcast.16, f32[1024,128]{1,0:T(8,128)} %bitcast.17, f32[1024,128]{1,0:T(8,128)} %bitcast.18), custom_call_target="tpu_custom_call" | custom-call | tf_op jit(solution)/shard_map/pallas_call | solution.py:491
  131.0 0.0 copy-start
  131.0 2.4 %copy.11 = f32[64,32,64]{2,1,0:T(8,128)} copy(f32[64,32,64]{2,1,0:T(8,128)} %get-tuple-element.4) | data formatting | bytes 1048576
  133.4 0.0 copy-done
  133.4 1.0 copy.12
  (2 shorter events, 0.0 us)
Async XLA Ops:
  0.6 0.7 copy-start.1
  131.0 2.4 %copy-start = (f32[64,32,64]{2,1,0:T(8,128)S(1)}, f32[64,32,64]{2,1,0:T(8,128)}, u32[]{:S(2)}) copy-start(f32[64,32,64]{2,1,0:T(8,128)} %get-tuple-element.5) | copy-start | bytes 1572868

commit v8 on v7

--- a/solution.py
+++ b/solution.py
@@ -143,6 +143,7 @@
 
     send_pieces(0)
     send_pieces(1)
+    send_pieces(2)
     got_place[me] = place_ref[...]
 
     @pl.loop(1, members)
@@ -339,7 +340,6 @@
         return (row_ids() // st + lane_ids() // st + x + colour) % 2 == 0
 
     forward(0)
-    send_pieces(2)
     forward(1)
     unpack(0, bv, 1)
     level_pass(PLANES, 1, lambda xs, hoods: [bv[x + 1] for x in xs])

time: 135 us -> 134 us (level)
  no operation moved by 1% of the time
where the time goes in v8:
time: 134 us
  Pallas kernels  129 us (96%)
  local copies, waits for them, and re-layouts  4.72 us (4%)
    pallas_call x1, Pallas kernels, body(): pl.pallas_call(functools.partial(kernel, sizes), out_shape=[jax.ShapeDtyp...  129 us
    unnamed x6, local copies, waits for them, and re-layouts  3.97 us

profile of v8, /device:TPU:0, one launch (start us, length us, event | category | flops | bytes accessed | tf_op | source)
XLA Modules:
  0.0 134.3 jit_solution(8375460956904415594)
XLA Ops:
  0.6 0.0 copy-start.1
  0.6 0.6 copy-done.1
  1.3 0.1 broadcast_in_dim_tile.3
  1.4 0.7 broadcast_in_dim.11.place_ref
  2.0 128.9 %shard_map.59 = (f32[64,32,64]{2,1,0:T(8,128)}, f32[64,32,64]{2,1,0:T(8,128)}) custom-call(s32[8,128]{1,0:T(8,128)} %broadcast_in_dim.11.place_ref, f32[1024,128]{1,0:T(8,128)} %bitcast.16, f32[1024,128]{1,0:T(8,128)} %bitcast.17, f32[1024,128]{1,0:T(8,128)} %bitcast.18), custom_call_target="tpu_custom_call" | custom-call | tf_op jit(solution)/shard_map/pallas_call | solution.py:491
  131.0 0.0 copy-start
  131.0 2.4 %copy.11 = f32[64,32,64]{2,1,0:T(8,128)} copy(f32[64,32,64]{2,1,0:T(8,128)} %get-tuple-element.4) | data formatting | bytes 1048576
  133.3 0.0 copy-done
  133.3 1.0 copy.12
  (2 shorter events, 0.0 us)
Async XLA Ops:
  0.6 0.7 copy-start.1
  131.0 2.4 %copy-start = (f32[64,32,64]{2,1,0:T(8,128)S(1)}, f32[64,32,64]{2,1,0:T(8,128)}, u32[]{:S(2)}) copy-start(f32[64,32,64]{2,1,0:T(8,128)} %get-tuple-element.5) | copy-start | bytes 1572868

commit v9 on v8

--- a/solution.py
+++ b/solution.py
@@ -458,8 +458,7 @@
             c, nb = hood
             r = rh[x] - (dg[x] * c - nb)
             for out, n in ((sol_out, c), (res_out, r)):
-                out[x] = n[:, :NZ]
-                out[x + PLANES] = pltpu.roll(n, NZ, 1)[:, :NZ]
+                out[x] = n
 
     halo_pass(v, 12, PLANES, 1, fine_faces, finish, staged=False)
 
@@ -488,9 +487,9 @@
         box = pltpu.VMEM((members, 4 * rows, LANES), F32)
         boxes = pltpu.VMEM((3, members, 4 * rows, LANES), F32)
         dma = pltpu.SemaphoreType.DMA
-        return pl.pallas_call(
+        packed = pl.pallas_call(
             functools.partial(kernel, sizes),
-            out_shape=[jax.ShapeDtypeStruct((NX, NY, NZ), F32)] * 2,
+            out_shape=[jax.ShapeDtypeStruct((PLANES, NY, LANES), F32)] * 2,
             in_specs=[pl.BlockSpec(memory_space=pltpu.VMEM)] + [pl.BlockSpec(memory_space=pltpu.HBM)] * 3,
             out_specs=[pl.BlockSpec(memory_space=pltpu.VMEM)] * 2,
             scratch_shapes=[
@@ -523,6 +522,7 @@
                 collective_id=0, has_side_effects=True, vmem_limit_bytes=60 * 1024 * 1024
             ),
         )(spot, rows128(rhs_boxes), rows128(a_boxes), rows128(b_boxes))
+        return tuple(jnp.concatenate([p[..., :NZ], p[..., NZ:]], axis=0) for p in packed)
 
     return jax.shard_map(
         body,

time: 134 us -> 135 us (level)
  other arithmetic: 0.01 us -> 2.13 us
  local copies, waits for them, and re-layouts: 4.72 us -> 3.31 us
    unnamed x6 -> x2, local copies, waits for them, and re-layouts: 3.97 us -> 0.65 us
    concatenate x0 -> x2, other arithmetic: none -> 2.12 us  [body(): jnp.concatenate([p[..., :NZ], p[..., NZ:]], axis=0)]
    slice x0 -> x1, local copies, waits for them, and re-layouts: none -> 1.91 us  [body(): p[..., :NZ]]
where the time goes in v9:
time: 135 us; the launch traced here: 134 us
  Pallas kernels  128 us (95%)
  local copies, waits for them, and re-layouts  3.31 us (2%)
  other arithmetic  2.13 us (2%)
    pallas_call x1, Pallas kernels, body(): pl.pallas_call(functools.partial(kernel, sizes), out_shape=[jax.ShapeDtyp...  128 us

profile of v9, /device:TPU:0, one launch (start us, length us, event | category | flops | bytes accessed | tf_op | source)
XLA Modules:
  0.0 134.3 jit_solution(1409824665309177904)
XLA Ops:
  0.6 0.0 copy-start
  0.6 0.6 copy-done
  1.3 0.1 broadcast_in_dim_tile.3
  1.4 0.7 broadcast_in_dim.11.place_ref
  2.0 128.2 %shard_map.59 = (f32[32,32,128]{2,1,0:T(8,128)}, f32[32,32,128]{2,1,0:T(8,128)}) custom-call(s32[8,128]{1,0:T(8,128)} %broadcast_in_dim.11.place_ref, f32[1024,128]{1,0:T(8,128)} %bitcast.16, f32[1024,128]{1,0:T(8,128)} %bitcast.17, f32[1024,128]{1,0:T(8,128)} %bitcast.18), custom_call_target="tpu_custom_call" | custom-call | tf_op jit(solution)/shard_map/pallas_call | solution.py:490
  130.3 1.9 %fusion = (f32[32,32,64]{2,1,0:T(8,128)S(1)}, f32[32,32,64]{2,1,0:T(8,128)S(1)}, f32[32,32,64]{2,1,0:T(8,128)S(1)}, f32[32,32,64]{2,1,0:T(8,128)S(1)}) fusion(f32[32,32,128]{2,1,0:T(8,128)} %get-tuple-element.5, f32[32,32,128]{2,1,0:T(8,128)} %get-tuple-element.4), kind=kLoop, calls=%fused_computation.3 | loop fusion | bytes 2097152 | tf_op jit(solution)/shard_map/slice | solution.py:525
  132.2 1.1 pad_maximum_fusion.1
  133.3 1.1 pad_maximum_fusion
  (2 shorter events, 0.0 us)
Async XLA Ops:
  0.6 0.7 copy-start
